TPU v7x, 128 devices: a whole 4x4x4 slice. The times are simulated.
128 devices in a mesh: dom: 32 (over x, y, core), tp: 4 (over z).
Axes of the slice: x: 4, y: 4, z: 4, core: 2. Of those that a mesh axis runs over, the one named last changes fastest.
Arguments:
- particle_suffix_cache: bfloat16 [2, 512, 512, 1024], P(None, 'dom', None, 'tp'), may hold values from -480 to 480
- hidden: bfloat16 [512, 2, 4096], P('dom'), may hold values from -6 to 6
- query_weight: bfloat16 [4096, 4096], P(None, 'tp'), may hold values from -0.09375 to 0.09375
- key_projection_weight: bfloat16 [4096, 1024], P(None, 'tp'), may hold values from -0.09375 to 0.09375
- value_projection_weight: bfloat16 [4096, 1024], P(None, 'tp'), may hold values from -0.09375 to 0.09375
- twist_weight: float32 [4096], P('tp'), may hold values from -6 to 6
- parent_twist: float32 [512], P('dom'), may hold values from -8 to 8
- log_ratio: float32 [512, 2], P('dom'), may hold values from -400 to 8
- ancestors: int32 [512], replicated, may hold values from 0 to 511, as said below
Outputs:
- resampled_cache: bfloat16 [2, 512, 512, 1024], P(None, 'dom', None, 'tp')
- fresh_token_entries: bfloat16 [2, 512, 2, 1024], P(None, 'dom', None, 'tp')
- attention: bfloat16 [512, 2, 4096], P('dom', None, 'tp')
- log_weights: float32 [512], P('dom')
Inputs may be any that keep to these rules, and one draw needn't show every extreme that they name: An old particle's index that lies on the new particle's own index of dom or on one of the two beside it: ancestors[n] // 16 differs from n // 16 by at most one; offspring counts are uneven.
All inputs are finite; a program needn't handle non-finite values.
Results may differ from a plain program's by a relative error of at most 0.007.
The roundings to bfloat16 on the way count: a program that leaves them out, or rounds other values in their place, can miss the bound.
Values may be sent and summed in bfloat16 or wider, within the bound.
No kernel may reach another device: no remote copies, remote signals or barrier semaphores. Data moves between devices by JAX's collectives and lax.ppermute only.
A program may use at most 192 MiB of HBM per device.

v0:
```python
import math

import jax
import jax.numpy as jnp
from jax import lax
from jax.sharding import PartitionSpec as P

HEAD_SIZE = 128
DECODE_STEPS = 2


ROPE_BASE = 500000.0


def extended_2(x, sides, width):
    for axis, dim in sides:
        peers, length = (lax.axis_size(axis), x.shape[dim])
        up = [(i, (i + 1) % peers) for i in range(peers - 1)]
        down = [(j, i) for i, j in up]
        last = lax.slice_in_dim(x, length - width, length, axis=dim)
        initial = lax.slice_in_dim(x, 0, width, axis=dim)
        before = lax.ppermute(last, axis, up)
        after = lax.ppermute(initial, axis, down)
        x = jnp.concatenate([before, x, after], axis=dim)
    return x


def combined_all(part, axis, combine):
    gathered = jax.tree.map(lambda a: lax.all_gather(a, axis), part)

    def take(source):
        return jax.tree.map(lambda a: lax.dynamic_index_in_dim(a, source, 0, False), gathered)

    return lax.fori_loop(
        1, lax.axis_size(axis), lambda source, state: combine(state, take(source)), take(0)
    )


def apply_rotary(tensor, anchor_point):
    half_dim = tensor.shape[-1] // 2
    step_count = tensor.shape[-3]
    positions = (anchor_point + jnp.arange(step_count)).astype(jnp.float32)
    frequency = jnp.exp(
        jnp.arange(half_dim).astype(jnp.float32) * (-2.0 * math.log(ROPE_BASE) / tensor.shape[-1])
    )
    angles = (positions[:, None] * frequency[None, :])[:, None, :]
    cosine = jnp.cos(angles)
    sine = jnp.sin(angles)
    first_half = tensor[..., :half_dim]
    second_half = tensor[..., half_dim:]
    return jnp.concatenate(
        [first_half * cosine - second_half * sine, first_half * sine + second_half * cosine], -1
    )


def project_tokens(rows, weight):
    flat = rows.reshape(-1, rows.shape[-1])
    return jnp.dot(flat, weight, preferred_element_type=jnp.float32).reshape(
        rows.shape[0], rows.shape[1], -1
    )


def finish(query_vectors, weighted, maxima, totals, fresh_keys, fresh_values):
    score_scale = 1.0 / math.sqrt(query_vectors.shape[-1])
    new_scores = (
        jnp.einsum(
            "ntkgd,nukd->ntkgu", query_vectors, fresh_keys, preferred_element_type=jnp.float32
        )
        * score_scale
    )
    step_count = query_vectors.shape[1]
    causal = jnp.arange(step_count)[:, None] >= jnp.arange(step_count)[None, :]
    new_scores = jnp.where(causal[None, :, None, None, :], new_scores, -jnp.inf)
    peak_score = jnp.maximum(maxima, jnp.max(new_scores, -1))
    carried = jnp.exp(maxima - peak_score)
    fresh = jnp.exp(new_scores - peak_score[..., None])
    numerator = carried[..., None] * weighted + jnp.einsum(
        "ntkgu,nukd->ntkgd",
        fresh,
        fresh_values.astype(jnp.float32),
        precision=lax.Precision.HIGHEST,
    )
    denominator = carried * totals + jnp.sum(fresh, -1)
    return numerator / denominator[..., None]


def attend(grouped, key_rows, value_rows):
    score_scale = 1.0 / math.sqrt(grouped.shape[-1])
    scores = (
        jnp.einsum("rtkgd,rlkd->rtkgl", grouped, key_rows, preferred_element_type=jnp.float32)
        * score_scale
    )
    maxima = jnp.max(scores, -1)
    expo = jnp.exp(scores - maxima[..., None])
    totals = jnp.sum(expo, -1)
    weighted = jnp.einsum(
        "rtkgl,rlkd->rtkgd",
        expo.astype(jnp.bfloat16),
        value_rows,
        preferred_element_type=jnp.float32,
    )
    return (weighted, maxima, totals)


def combine_mass(earlier, later):
    joined = jnp.maximum(earlier[0], later[0])
    return (
        joined,
        earlier[1] * jnp.exp(earlier[0] - joined) + later[1] * jnp.exp(later[0] - joined),
    )


def shards(
    particle_suffix_cache,
    hidden,
    query_weight,
    key_projection_weight,
    value_projection_weight,
    twist_weight,
    parent_twist,
    log_ratio,
    ancestors,
):
    per_device = hidden.shape[0]
    local_heads = query_weight.shape[1] // HEAD_SIZE
    local_groups = key_projection_weight.shape[1] // HEAD_SIZE
    query_group_size = local_heads // local_groups
    anchor_point = particle_suffix_cache.shape[2]
    query_vectors = apply_rotary(
        project_tokens(hidden, query_weight).reshape(
            per_device, DECODE_STEPS, local_heads, HEAD_SIZE
        ),
        anchor_point,
    ).astype(jnp.bfloat16)
    fresh_keys = apply_rotary(
        project_tokens(hidden, key_projection_weight).reshape(
            per_device, DECODE_STEPS, local_groups, HEAD_SIZE
        ),
        anchor_point,
    ).astype(jnp.bfloat16)
    fresh_values = (
        project_tokens(hidden, value_projection_weight)
        .reshape(per_device, DECODE_STEPS, local_groups, HEAD_SIZE)
        .astype(jnp.bfloat16)
    )
    fresh_token_entries = jnp.stack(
        [
            fresh_keys.reshape(per_device, DECODE_STEPS, local_groups * HEAD_SIZE),
            fresh_values.reshape(per_device, DECODE_STEPS, local_groups * HEAD_SIZE),
        ]
    )
    grouped = query_vectors.reshape(
        per_device, DECODE_STEPS, local_groups, query_group_size, HEAD_SIZE
    )
    first = lax.axis_index("dom") * per_device
    mine = lax.dynamic_slice_in_dim(ancestors, first, per_device)
    extended = extended_2(particle_suffix_cache, (("dom", 1),), per_device)
    pick_near = mine - first + per_device
    resampled_cache = jnp.take(extended, pick_near, axis=1)
    key_rows = resampled_cache[0].reshape(per_device, anchor_point, local_groups, HEAD_SIZE)
    value_rows = resampled_cache[1].reshape(per_device, anchor_point, local_groups, HEAD_SIZE)
    weighted, maxima, totals = attend(grouped, key_rows, value_rows)
    near_twist = extended_2(parent_twist, (("dom", 0),), per_device)
    parent_value = jnp.take(near_twist, pick_near)
    outputs = finish(grouped, weighted, maxima, totals, fresh_keys, fresh_values)
    attention = outputs.reshape(per_device, DECODE_STEPS, local_heads * HEAD_SIZE).astype(
        jnp.bfloat16
    )
    partial_twist = jnp.sum(
        outputs[:, DECODE_STEPS - 1].reshape(per_device, local_heads * HEAD_SIZE)
        * twist_weight[None, :],
        1,
    )
    twist_value = lax.psum(partial_twist, "tp")
    log_weight = jnp.sum(log_ratio, 1) + twist_value - parent_value
    local_peak = jnp.max(log_weight)
    peak, mass = combined_all(
        (local_peak, jnp.sum(jnp.exp(log_weight - local_peak))), "dom", combine_mass
    )
    log_weights = log_weight - (peak + jnp.log(mass))
    return (resampled_cache, fresh_token_entries, attention, log_weights)


def solution(mesh):
    return jax.shard_map(
        shards,
        mesh=mesh,
        in_specs=(
            P(None, "dom", None, "tp"),
            P("dom", None, None),
            P(None, "tp"),
            P(None, "tp"),
            P(None, "tp"),
            P("tp"),
            P("dom"),
            P("dom", None),
            P(),
        ),
        out_specs=(
            P(None, "dom", None, "tp"),
            P(None, "dom", None, "tp"),
            P("dom", None, "tp"),
            P("dom"),
        ),
        check_vma=False,
    )
```

profile of v0, /device:TPU:0, one launch (start us, length us, event | category | flops | bytes accessed | tf_op | source)
XLA Modules:
  0.0 353.8 jit_solution(3889751997050621079)
XLA Ops:
  0.6 1.4 collective-permute-start.1
  2.1 6.2 %collective-permute-start = (bf16[2,16,512,256]{3,2,1,0:T(8,128)(2,1)}, bf16[2,16,512,256]{3,2,1,0:T(8,128)(2,1)}, u32[]{:S(2)}, u32[]{:S(2)}) collective-permute-start(bf16[2,16,512,256]{3,2,1,0:T(8,128)(2,1)} %param.11), channel_id=1, source_target_pairs={{0,4},{4,8},{8,12},{12,16},{16,20},{20,24},{24,28},{28,32},{32,36}... | collective-permute-start | bytes 25165832 | tf_op jit(solution)/shard_map/ppermute | solution.py:22
  8.3 1.3 collective-permute-start.3
  9.6 3.0 collective-permute-start.2
  12.7 2.9 copy.55
  15.6 1.7 convolution_convert_fusion
  17.3 2.9 copy.52
  20.4 0.7 fusion.13
  22.0 11.9 %copy.60 = bf16[1024,4096]{1,0:T(8,128)(2,1)} copy(bf16[1024,4096]{0,1:T(8,128)(2,1)} %bitcast.73) | data formatting | bytes 16777216 | tf_op jit(solution)/shard_map/dot_general | solution.py:58
  33.9 6.0 %fusion.10 = f32[16,2,8,128]{3,0,2,1:T(8,128)S(1)} fusion(bf16[8,128,4096,1]{2,1,0,3:T(8,128)(2,1)} %bitcast.71, bf16[16,2,4096,1]{2,1,0,3:T(2,128)(2,1)S(1)} %bitcast.79), kind=kOutput, calls=%fused_computation.19 | convolution fusion | flops 268435456 | bytes 8781824 | tf_op jit(solution)/shard_map/dot_general | solution.py:58
  40.2 0.8 compare_and_fusion
  41.0 0.8 fusion.23
  43.2 17.6 %pad_maximum_fusion = bf16[2,48,512,256]{3,2,1,0:T(8,128)(2,1)} fusion(bf16[2,16,512,256]{3,2,1,0:T(8,128)(2,1)} %collective-permute-done.1, bf16[2,16,512,256]{3,2,1,0:T(8,128)(2,1)} %param.11, bf16[2,16,512,256]{3,2,1,0:T(8,128)(2,1)} %collective-permute-done), kind=kLoop, calls=%fused_computation.2 | loop fusion | flops 25165824 | bytes 50331648 | tf_op jit(solution)/shard_map/concatenate | solution.py:24
  60.8 13.1 %gather_fusion = bf16[16,2,512,256]{3,2,1,0:T(8,128)(2,1)} fusion(bf16[2,48,512,256]{3,2,1,0:T(8,128)(2,1)} %pad_maximum_fusion, s32[1024]{0:T(1024)S(1)} %pad_clamp_fusion), kind=kCustom, calls=%fused_computation | custom fusion | bytes 16777280 | tf_op jit(solution)/shard_map/jit(_take)/gather | solution.py:159
  73.9 7.5 %select_bitcast_fusion = bf16[2,16,512,256]{3,2,0,1:T(8,128)(2,1)} fusion(bf16[16,2,512,256]{3,2,1,0:T(8,128)(2,1)} %gather_fusion, pred[16]{0:T(512)(128)(4,1)S(1)} %get-tuple-element.159), kind=kLoop, calls=%fused_computation.3 | loop fusion | flops 4194304 | bytes 16777232 | tf_op jit(solution)/shard_map/jit(_take)/select_n | solution.py:159
  81.4 7.7 %copy.40 = bf16[2,16,512,256]{3,2,1,0:T(8,128)(2,1)} copy(bf16[2,16,512,256]{3,2,0,1:T(8,128)(2,1)} %select_bitcast_fusion) | data formatting | bytes 16777216
  89.0 5.8 %fusion.21 = (bf16[1,16,512,256]{3,2,0,1:T(8,128)(2,1)}, bf16[1,16,512,256]{3,2,0,1:T(8,128)(2,1)}) fusion(bf16[2,16,512,256]{3,2,0,1:T(8,128)(2,1)} %select_bitcast_fusion), kind=kLoop, calls=%fused_computation.53 | loop fusion | bytes 16777216 | tf_op jit(solution)/shard_map/slice | solution.py:161
  94.8 6.4 %copy.29 = bf16[1,16,512,256]{2,3,1,0:T(8,128)(2,1)} copy(bf16[1,16,512,256]{3,2,0,1:T(8,128)(2,1)} %get-tuple-element.162) | data formatting | bytes 8388608 | tf_op jit(solution)/shard_map/slice | solution.py:160
  101.2 3.0 fusion.22
  105.2 6.4 %copy.36 = bf16[1,16,512,256]{2,3,1,0:T(8,128)(2,1)} copy(bf16[1,16,512,256]{3,2,0,1:T(8,128)(2,1)} %get-tuple-element.161) | data formatting | bytes 8388608 | tf_op jit(solution)/shard_map/slice | solution.py:161
  111.7 3.4 fusion.24
  116.0 11.8 %psum.7 = f32[16]{0:T(128)S(1)} all-reduce(f32[16]{0:T(128)S(1)} %fusion.15), channel_id=1, replica_groups=mesh['dom'=32,'tp'=4] {'tp'}, use_global_device_ids=true, to_apply=%region_6.7 | all-reduce | flops 16 | bytes 128 | tf_op jit(solution)/shard_map/psum | solution.py:174
  128.5 1.3 exponential_reduce_fusion
  129.8 1.4 dynamic-update-slice
  131.2 1.5 dynamic-update-slice.1
  132.7 117.9 %all-reduce.2 = (f32[32]{0:T(128)S(1)}, f32[32]{0:T(128)S(1)}) all-reduce(f32[32]{0:T(128)S(1)} %dynamic-update-slice, f32[32]{0:T(128)S(1)} %dynamic-update-slice.1), channel_id=1, replica_groups=mesh['dom'=32,'tp'=4] {'dom'}, use_global_device_ids=true, to_apply=%add | all-reduce | flops 64 | bytes 512
  250.7 102.5 %while.17 = (s32[]{:T(128)}, f32[]{:T(128)}, f32[]{:T(128)}, f32[32]{0:T(128)S(1)}, f32[32]{0:T(128)S(1)}, /*index=5*/s32[]{:T(128)}, s32[]{:T(128)}, s32[]{:T(128)}) while((s32[]{:T(128)}, f32[]{:T(128)}, f32[]{:T(128)}, f32[32]{0:T(128)S(1)}, f32[32]{0:T(128)S(1)}, /*index=5*/s32[]{:T(128)}, s32[]{:T(128)}, s32[]{:T(128)}) %tuple.51), condition=%wide.region_10.11_spmd, body=%wide.region_9.10_spmd.sunk | while | flops 11 | bytes 247 | solution.py:34
  250.7 0.7 dynamic_slice.37
  254.0 0.7 dynamic_slice.37
  267.3 0.7 dynamic_slice.37
  306.9 0.7 dynamic_slice.37
  330.1 0.7 dynamic_slice.37
  (104 shorter events, 41.1 us)
Async XLA Ops:
  0.6 19.8 %copy-start = (bf16[16,2,4096]{2,1,0:T(2,128)(2,1)S(1)}, bf16[16,2,4096]{2,1,0:T(2,128)(2,1)}, u32[]{:S(2)}) copy-start(bf16[16,2,4096]{2,1,0:T(2,128)(2,1)} %param.12) | copy-start | bytes 786436
  0.6 42.6 %collective-permute-start.1 = (bf16[2,16,512,256]{3,2,1,0:T(8,128)(2,1)}, bf16[2,16,512,256]{3,2,1,0:T(8,128)(2,1)}, u32[]{:S(2)}, u32[]{:S(2)}) collective-permute-start(bf16[2,16,512,256]{3,2,1,0:T(8,128)(2,1)} %param.11), channel_id=1, source_target_pairs={{4,0},{8,4},{12,8},{16,12},{20,16},{24,20},{28,24},{32,28},{36,32}... | collective-permute-start | bytes 25165832 | tf_op jit(solution)/shard_map/ppermute | solution.py:23
  2.1 41.1 %collective-permute-start = (bf16[2,16,512,256]{3,2,1,0:T(8,128)(2,1)}, bf16[2,16,512,256]{3,2,1,0:T(8,128)(2,1)}, u32[]{:S(2)}, u32[]{:S(2)}) collective-permute-start(bf16[2,16,512,256]{3,2,1,0:T(8,128)(2,1)} %param.11), channel_id=1, source_target_pairs={{0,4},{4,8},{8,12},{12,16},{16,20},{20,24},{24,28},{28,32},{32,36}... | collective-permute-start | bytes 25165832 | tf_op jit(solution)/shard_map/ppermute | solution.py:22
  8.3 34.1 %collective-permute-start.3 = (f32[16]{0:T(128)}, f32[16]{0:T(128)S(1)}, u32[]{:S(2)}, u32[]{:S(2)}) collective-permute-start(f32[16]{0:T(128)} %param.17), channel_id=1, source_target_pairs={{4,0},{8,4},{12,8},{16,12},{20,16},{24,20},{28,24},{32,28},{36,32}... | collective-permute-start | bytes 200 | tf_op jit(solution)/shard_map/ppermute | solution.py:23
  9.6 32.9 %collective-permute-start.2 = (f32[16]{0:T(128)}, f32[16]{0:T(128)S(1)}, u32[]{:S(2)}, u32[]{:S(2)}) collective-permute-start(f32[16]{0:T(128)} %param.17), channel_id=1, source_target_pairs={{0,4},{4,8},{8,12},{12,16},{16,20},{20,24},{24,28},{28,32},{32,36}... | collective-permute-start | bytes 200 | tf_op jit(solution)/shard_map/ppermute | solution.py:22
  33.9 6.2 %copy-start.2 = (f32[16,2]{0,1:T(2,128)S(1)}, f32[16,2]{0,1:T(2,128)}, u32[]{:S(2)}) copy-start(f32[16,2]{0,1:T(2,128)} %param.18) | copy-start | bytes 388
  33.9 7.9 %copy-start.4 = (u32[128]{0:T(128)S(1)}, u32[128]{0:T(128)}, u32[]{:S(2)}) copy-start(u32[128]{0:T(128)} %constant.103) | copy-start | bytes 1540
  33.9 8.5 %copy-start.3 = (f32[16]{0:T(128)S(1)}, f32[16]{0:T(128)}, u32[]{:S(2)}) copy-start(f32[16]{0:T(128)} %param.17) | copy-start | bytes 196
  104.7 11.1 %copy-start.1 = (f32[1024]{0:T(1024)S(1)}, f32[1024]{0:T(1024)}, u32[]{:S(2)}) copy-start(f32[1024]{0:T(1024)} %param.16) | copy-start | bytes 12292
where the time goes:
time: 357 us; the launch traced here: 354 us
  blocking collectives  130 us (36%)
  local copies, waits for them, and re-layouts  102 us (29%)
  loops' own time  63.8 us (18%)
  other arithmetic  29.7 us (8%)
  matrix products  16 us (4%)
  starting transfers between devices  12 us (3%)
    unnamed x1, blocking collectives  118 us
    another operation x1, loops' own time, combined_all(): lax.fori_loop(1, lax.axis_size(axis), lambda source, state: combine(state...  63.8 us
    dynamic_slice x62, local copies, waits for them, and re-layouts, take(): lax.dynamic_index_in_dim(a, source, 0, False)  38.7 us
    dot_general x3, local copies, waits for them, and re-layouts, project_tokens(): jnp.dot(flat, weight, preferred_element_type=jnp.float32)  17.7 us
    concatenate x2, other arithmetic, extended_2(): x = jnp.concatenate([before, x, after], axis=dim)  17.7 us
    gather x1, local copies, waits for them, and re-layouts, shards(): resampled_cache = jnp.take(extended, pick_near, axis=1)  13.1 us
    unnamed x19, local copies, waits for them, and re-layouts  12.6 us
    slice x2, local copies, waits for them, and re-layouts, shards(): resampled_cache[1]  12.2 us
  transfers between devices with their start and end apart: 4, of which 0 were waited for; matrix products, arithmetic and copies ran while one was open for 9% of the time, Pallas kernels for 0%

commit v1 on v0

v1 whole, which is shorter than its diff:
```python
import functools
import math

import jax
import jax.numpy as jnp
import numpy as np
from jax import lax
from jax.experimental import pallas as pl
from jax.experimental.pallas import tpu as pltpu
from jax.sharding import PartitionSpec as P

HEAD_SIZE = 128
DECODE_STEPS = 2
ROPE_BASE = 500000.0
PIECES = (8,)
ALWAYS = sum(PIECES)
AT_ONCE = 4

SMEM = pl.BlockSpec(memory_space=pltpu.SMEM)
VMEM = pl.BlockSpec(memory_space=pltpu.VMEM)
ANY = pl.BlockSpec(memory_space=pl.ANY)
LIGHT = pl.CostEstimate(flops=0, bytes_accessed=0, transcendentals=0)


def chip_mate(d):
    return d + 1 - 2 * (d % 2)


def next_chip(d):
    return d - 1 + 2 * (d % 2)


def rope_tables(rows, anchor_point):
    half = HEAD_SIZE // 2
    frequency = np.exp(
        np.arange(half, dtype=np.float32) * np.float32(-2.0 * math.log(ROPE_BASE) / HEAD_SIZE)
    ).astype(np.float32)
    positions = (anchor_point + np.arange(rows) % DECODE_STEPS).astype(np.float32)
    angles = (positions[:, None] * frequency[None, :]).astype(np.float32)
    cosine = np.cos(angles).astype(np.float32)
    sine = np.sin(angles).astype(np.float32)
    return np.concatenate([cosine, cosine], 1), np.concatenate([-sine, sine], 1)


def bit_count(mask):
    mask = mask - ((mask >> 1) & 0x55555555)
    mask = (mask & 0x33333333) + ((mask >> 2) & 0x33333333)
    mask = (mask + (mask >> 4)) & 0x0F0F0F0F
    return (mask * 0x01010101) >> 24


def plan_kernel(peers, per_device, ancestors, grid, count, picks, ranks):
    d = lax.axis_index("dom")
    shape = grid.shape
    flat = lax.broadcasted_iota(jnp.int32, shape, 0) * shape[1] + lax.broadcasted_iota(
        jnp.int32, shape, 1
    )
    home = flat // per_device
    offset = grid[...] - next_chip(home) * per_device
    inside = (offset >= 0) & (offset < per_device)
    bits = jnp.where(inside, jnp.int32(1) << (offset & (per_device - 1)), 0)
    shift = 1
    while shift < per_device:
        bits = bits | pltpu.roll(bits, shape[1] - shift, 1)
        shift *= 2
    most = jnp.where(flat % per_device == 0, bit_count(bits), 0)
    count[0] = jnp.max(most.astype(jnp.float32)).astype(jnp.int32)

    def needed(home, owner):
        mask = jnp.int32(0)
        for k in range(per_device):
            offset = ancestors[home * per_device + k] - owner * per_device
            inside = (offset >= 0) & (offset < per_device)
            mask = mask | jnp.where(inside, jnp.int32(1) << (offset & (per_device - 1)), 0)
        return mask

    there = next_chip(d)
    mask = needed(jnp.clip(there, 0, peers - 1), d)
    position = jnp.int32(0)
    for j in range(per_device):
        picks[j] = 0
    for j in range(per_device):
        picks[position] = j
        position = position + ((mask >> j) & 1)
    mask = needed(d, there)
    for k in range(per_device):
        offset = ancestors[d * per_device + k] - there * per_device
        inside = (offset >= 0) & (offset < per_device)
        below = (jnp.int32(1) << (offset & (per_device - 1))) - 1
        ranks[k] = jnp.where(inside, bit_count(mask & below), -1)


def plan(ancestors, peers, per_device):
    return pl.pallas_call(
        functools.partial(plan_kernel, peers, per_device),
        out_shape=(
            jax.ShapeDtypeStruct((1,), jnp.int32),
            jax.ShapeDtypeStruct((per_device,), jnp.int32),
            jax.ShapeDtypeStruct((per_device,), jnp.int32),
        ),
        in_specs=[SMEM, VMEM],
        out_specs=(SMEM, SMEM, SMEM),
        cost_estimate=LIGHT,
        name="plan",
    )(ancestors, ancestors.reshape(-1, 128))


def gather_kernel(skip, size, picks, cache, sent, held, loads, stores):
    def load(i, c):
        return pltpu.make_async_copy(cache.at[c, picks[skip + i]], held.at[c, i], loads.at[c, i])

    def store(i, c):
        return pltpu.make_async_copy(held.at[c, i], sent.at[c, i], stores.at[c, i])

    def each(act):
        def body(i, carry):
            for c in range(2):
                act(i, c)
            return carry

        lax.fori_loop(0, size, body, 0)

    each(lambda i, c: load(i, c).start())

    def forward(i, c):
        load(i, c).wait()
        store(i, c).start()

    each(forward)
    each(lambda i, c: store(i, c).wait())


def gather(picks, cache, skip, size):
    shape = (2, size, *cache.shape[2:])
    return pl.pallas_call(
        functools.partial(gather_kernel, skip, size),
        out_shape=jax.ShapeDtypeStruct(shape, cache.dtype),
        in_specs=[SMEM, ANY],
        out_specs=ANY,
        scratch_shapes=[
            pltpu.VMEM(shape, cache.dtype),
            pltpu.SemaphoreType.DMA((2, size)),
            pltpu.SemaphoreType.DMA((2, size)),
        ],
        compiler_params=pltpu.CompilerParams(vmem_limit_bytes=20 * 2**20),
        cost_estimate=LIGHT,
        name="gather",
    )(picks, cache)


def place_kernel(per_device, find, numbers, *refs):
    *sources, out, held, loads, stores = refs
    d = lax.axis_index("dom")

    def each(act):
        def body(k, carry):
            for source, (there, at) in zip(sources, find(numbers, d, k)):

                @pl.when(there)
                def _():
                    for c in range(2):
                        act(source, at, k, c)

            return carry

        lax.fori_loop(0, per_device, body, 0)

    def load(source, at, k, c):
        return pltpu.make_async_copy(source.at[c, at], held.at[c, k], loads.at[c, k])

    def store(k, c):
        return pltpu.make_async_copy(held.at[c, k], out.at[c, k], stores.at[c, k])

    def forward(source, at, k, c):
        load(source, at, k, c).wait()
        store(k, c).start()

    each(lambda source, at, k, c: load(source, at, k, c).start())
    each(forward)
    each(lambda source, at, k, c: store(k, c).wait())


def place(find, numbers, sources, placed, name):
    per_device = placed.shape[1]
    operands = [numbers, *sources, placed]

    def kernel(*refs):
        refs = list(refs)
        del refs[1 + len(sources)]
        place_kernel(per_device, find, *refs)

    return pl.pallas_call(
        kernel,
        out_shape=pltpu.HBM(placed.shape, placed.dtype),
        in_specs=[SMEM] + [ANY] * (len(operands) - 1),
        out_specs=ANY,
        scratch_shapes=[
            pltpu.VMEM(placed.shape, placed.dtype),
            pltpu.SemaphoreType.DMA((2, per_device)),
            pltpu.SemaphoreType.DMA((2, per_device)),
        ],
        input_output_aliases={len(operands) - 1: 0},
        compiler_params=pltpu.CompilerParams(vmem_limit_bytes=20 * 2**20),
        cost_estimate=LIGHT,
        name=name,
    )(*operands)


def place_mate(ancestors, mate, placed):
    per_device = placed.shape[1]

    def find(ancestors, d, k):
        offset = ancestors[d * per_device + k] - chip_mate(d) * per_device
        yield (offset >= 0) & (offset < per_device), offset

    return place(find, ancestors, [mate], placed, "place_mate")


def place_far(ranks, came, placed, skip):
    size = came.shape[1]

    def find(ranks, d, k):
        rank = ranks[k] - skip
        yield (rank >= 0) & (rank < size), rank

    return place(find, ranks, [came], placed, "place_far")


def project_kernel(heads, groups, own, mate, far, wq, wk, wv, cosine, sine, *refs):
    *outs, keys, values, total, turned = refs
    step = pl.program_id(0)
    width_q, width_k = heads * HEAD_SIZE, groups * HEAD_SIZE
    rows = jnp.concatenate([own[...], mate[...], far[...]], 0)
    parts = (
        (wq, 0, width_q),
        (wk, width_q, width_k),
        (wv, width_q + width_k, width_k),
    )

    @pl.when(step == 0)
    def _():
        total[...] = jnp.zeros_like(total)

    for weight, at, width in parts:
        total[:, at : at + width] += jnp.dot(
            rows, weight[...], preferred_element_type=jnp.float32
        )

    @pl.when(step == pl.num_programs(0) - 1)
    def _():
        count = own.shape[0]
        queries = heads * count

        def turn(x):
            return x * cosine[...] + pltpu.roll(x, HEAD_SIZE // 2, 1) * sine[...]

        for h, packed in enumerate(outs):
            mine = slice(h * count, (h + 1) * count)
            for i in range(heads):
                turned[:, i, :] = turn(total[mine, i * HEAD_SIZE : (i + 1) * HEAD_SIZE])
            packed[:queries, :] = turned[...].reshape(queries, HEAD_SIZE).astype(packed.dtype)
            for g in range(groups):
                lanes = slice(g * HEAD_SIZE, (g + 1) * HEAD_SIZE)
                at = width_q + g * HEAD_SIZE
                key = turn(total[mine, at : at + HEAD_SIZE]).astype(packed.dtype)
                at = at + width_k
                value = total[mine, at : at + HEAD_SIZE].astype(packed.dtype)
                at = queries + g * count
                packed[at : at + count, :] = key
                at = queries + (groups + g) * count
                packed[at : at + count, :] = value
                if h == 0:
                    keys[:, lanes] = key
                    values[:, lanes] = value


def project(own, mate, far, wq, wk, wv, anchor_point):
    count, depth = own.shape
    heads, groups = wq.shape[1] // HEAD_SIZE, wk.shape[1] // HEAD_SIZE
    block = 1024
    cosine, sine = rope_tables(count, anchor_point)
    columns = wq.shape[1] + wk.shape[1] + wv.shape[1]
    whole = lambda *shape: pl.BlockSpec(shape, lambda i: (0, 0))
    rows = pl.BlockSpec((count, block), lambda i: (0, i))
    packed = ((heads + 2 * groups) * count, HEAD_SIZE)
    fresh = (count, groups * HEAD_SIZE)
    return pl.pallas_call(
        functools.partial(project_kernel, heads, groups),
        grid=(depth // block,),
        out_shape=[jax.ShapeDtypeStruct(shape, jnp.bfloat16) for shape in (packed,) * 3 + (fresh,) * 2],
        in_specs=[
            rows,
            rows,
            rows,
            pl.BlockSpec((block, wq.shape[1]), lambda i: (i, 0)),
            pl.BlockSpec((block, wk.shape[1]), lambda i: (i, 0)),
            pl.BlockSpec((block, wv.shape[1]), lambda i: (i, 0)),
            whole(count, HEAD_SIZE),
            whole(count, HEAD_SIZE),
        ],
        out_specs=[whole(*shape) for shape in (packed,) * 3 + (fresh,) * 2],
        scratch_shapes=[
            pltpu.VMEM((3 * count, columns), jnp.float32),
            pltpu.VMEM((count, heads, HEAD_SIZE), jnp.float32),
        ],
        compiler_params=pltpu.CompilerParams(vmem_limit_bytes=56 * 2**20),
        cost_estimate=LIGHT,
        name="project",
    )(own, mate, far, wq, wk, wv, cosine, sine)


def attend_kernel(
    peers, per_device, heads, groups,
    ancestors, parent_twist, log_ratio, twist_weight, own, mate, far, cache,
    out_own, out_mate, out_far, part, placed,
    held, tokens, fresh, results, lists, slots, owners, sems, stores,
):
    d = lax.axis_index("dom")
    first_lane = (lax.axis_index("tp") == 0).astype(jnp.float32)
    tile = DECODE_STEPS * heads
    queries = per_device * tile
    small = per_device * DECODE_STEPS
    homes = (d, chip_mate(d), next_chip(d))

    def load(j, c):
        return pltpu.make_async_copy(cache.at[c, j], held.at[c, j], sems.at[c, j])

    def begin(j, carry):
        for c in range(2):
            load(j, c).start()
        lists[j] = -1
        return carry

    lax.fori_loop(0, per_device, begin, 0)
    for h, home in enumerate(homes):
        there = (home >= 0) & (home < peers)
        start = jnp.clip(home, 0, peers - 1) * per_device

        def enlist(k, carry):
            offset = ancestors[start + k] - d * per_device

            @pl.when(there & (offset >= 0) & (offset < per_device))
            def _():
                slot = h * per_device + k
                lists[per_device + slot] = lists[offset]
                lists[offset] = slot

            return carry

        lax.fori_loop(0, per_device, enlist, 0)

    def flatten(j, count):
        def step(state):
            slot, count = state
            slots[count] = slot
            owners[count] = j
            return lists[per_device + slot], count + 1

        return lax.while_loop(lambda state: state[0] >= 0, step, (lists[j], count))[1]

    count = lax.fori_loop(0, per_device, flatten, jnp.int32(0))
    for extra in range(AT_ONCE - 1):

        @pl.when(count > 0)
        def _():
            slots[count + extra] = slots[count - 1]
            owners[count + extra] = owners[count - 1]

    part[...] = jnp.zeros_like(part)
    part[3 * per_device :, :DECODE_STEPS] = log_ratio[...] * first_lane
    results[...] = jnp.zeros_like(results)
    for h, source in enumerate((own, mate, far)):
        tokens[h * queries : (h + 1) * queries, :] = source[:queries, :]
        size = source.shape[0] - queries
        fresh[h * size : (h + 1) * size, :] = source[queries:, :].astype(jnp.float32)
    block = 2 * groups * small
    row = lax.broadcasted_iota(jnp.int32, (tile, 1), 0)
    lower = (row % heads) < heads // groups
    later = row >= heads
    lane = lax.broadcasted_iota(jnp.int32, (1, HEAD_SIZE), 1)
    scale = 1.0 / math.sqrt(HEAD_SIZE)
    twist = jnp.concatenate([jnp.zeros_like(twist_weight), twist_weight[...]], 0)

    def by_group(at):
        pair = [fresh[pl.ds(at + g * small, 1), :] for g in range(groups)]
        return jnp.where(lower, pair[0], pair[1])

    def scores_of(j, slot):
        query = tokens[pl.ds(pl.multiple_of(slot * tile, tile), tile), :]
        none = jnp.zeros_like(query)
        wide = jnp.concatenate([jnp.where(lower, query, none), jnp.where(lower, none, query)], 1)
        scores = (
            lax.dot_general(
                wide, held[0, j], (((1,), (1,)), ((), ())), preferred_element_type=jnp.float32
            )
            * scale
        )
        return query.astype(jnp.float32), scores

    def weights_of(scores):
        maxima = jnp.max(scores, 1, keepdims=True)
        expo = jnp.exp(scores - maxima)
        return maxima, expo

    def finish(j, slot, query, maxima, totals, both):
        weighted = jnp.where(lower, both[:, :HEAD_SIZE], both[:, HEAD_SIZE:])
        at = (slot // per_device) * block + (slot % per_device) * DECODE_STEPS
        new = [
            jnp.sum(query * by_group(at + u), 1, keepdims=True) * scale
            for u in range(DECODE_STEPS)
        ]
        new[1] = jnp.where(later, new[1], -jnp.inf)
        peak = jnp.maximum(maxima, jnp.maximum(new[0], new[1]))
        carried = jnp.exp(maxima - peak)
        numerator = carried * weighted
        denominator = carried * totals
        for u in range(DECODE_STEPS):
            share = jnp.exp(new[u] - peak)
            numerator = numerator + share * by_group(at + groups * small + u)
            denominator = denominator + share
        outputs = numerator / denominator
        results[pl.ds(pl.multiple_of(slot * tile, tile), tile), :] = outputs.astype(jnp.bfloat16)
        twisted = jnp.sum(outputs * twist, 0, keepdims=True)
        less = jnp.where(lane == 0, parent_twist[j] * first_lane, 0.0)
        part[pl.ds(slot, 1), :] = twisted - less

    def store(k, c):
        offset = ancestors[d * per_device + k] - d * per_device
        return pltpu.make_async_copy(held.at[c, offset], placed.at[c, k], stores.at[c, k])

    def each_own(act):
        def body(k, carry):
            offset = ancestors[d * per_device + k] - d * per_device

            @pl.when((offset >= 0) & (offset < per_device))
            def _():
                for c in range(2):
                    act(store(k, c))

            return carry

        lax.fori_loop(0, per_device, body, 0)

    def arrive(j, carry):
        for c in range(2):
            load(j, c).wait()
        return carry

    def serve(step, loaded):
        at = step * AT_ONCE
        last = owners[at + AT_ONCE - 1] + 1
        lax.fori_loop(loaded, last, arrive, 0)
        jobs = [(owners[at + i], slots[at + i]) for i in range(AT_ONCE)]
        scored = [scores_of(*job) for job in jobs]
        weights = [weights_of(scores) for _, scores in scored]
        totals = [jnp.sum(expo, 1, keepdims=True) for _, expo in weights]
        both = [
            jnp.dot(expo.astype(jnp.bfloat16), held[1, job[0]], preferred_element_type=jnp.float32)
            for job, (_, expo) in zip(jobs, weights)
        ]
        for i, job in enumerate(jobs):
            finish(*job, scored[i][0], weights[i][0], totals[i], both[i])
        return last

    loaded = lax.fori_loop(0, (count + AT_ONCE - 1) // AT_ONCE, serve, jnp.int32(0))
    lax.fori_loop(loaded, per_device, arrive, 0)
    each_own(lambda copy: copy.start())
    for h, out in enumerate((out_own, out_mate, out_far)):
        out[...] = results[h * queries : (h + 1) * queries, :]
    each_own(lambda copy: copy.wait())


def attend(ancestors, parent_twist, log_ratio, twist_weight, own, mate, far, cache, peers, heads, groups):
    per_device = cache.shape[1]
    tile = DECODE_STEPS * heads
    queries = per_device * tile
    block = own.shape[0] - queries
    result = jax.ShapeDtypeStruct((queries, HEAD_SIZE), jnp.bfloat16)
    return pl.pallas_call(
        functools.partial(attend_kernel, peers, per_device, heads, groups),
        out_shape=(
            result,
            result,
            result,
            jax.ShapeDtypeStruct((4 * per_device, HEAD_SIZE), jnp.float32),
            pltpu.HBM(cache.shape, cache.dtype),
        ),
        in_specs=[SMEM, SMEM, VMEM, VMEM, VMEM, VMEM, VMEM, ANY],
        out_specs=(VMEM, VMEM, VMEM, VMEM, ANY),
        scratch_shapes=[
            pltpu.VMEM(cache.shape, cache.dtype),
            pltpu.VMEM((3 * queries, HEAD_SIZE), jnp.bfloat16),
            pltpu.VMEM((3 * block, HEAD_SIZE), jnp.float32),
            pltpu.VMEM((3 * queries, HEAD_SIZE), jnp.bfloat16),
            pltpu.SMEM((4 * per_device,), jnp.int32),
            pltpu.SMEM((3 * per_device + AT_ONCE,), jnp.int32),
            pltpu.SMEM((3 * per_device + AT_ONCE,), jnp.int32),
            pltpu.SemaphoreType.DMA((2, per_device)),
            pltpu.SemaphoreType.DMA((2, per_device)),
        ],
        compiler_params=pltpu.CompilerParams(vmem_limit_bytes=24 * 2**20),
        cost_estimate=LIGHT,
        name="attend",
    )(ancestors, parent_twist, log_ratio, twist_weight, own, mate, far, cache)


def normalise_kernel(terms, *refs):
    *parts, out = refs
    del terms
    total = parts[0][...]
    for part in parts[1:]:
        total = total + part[...]
    peak = jnp.max(total, keepdims=True)
    mass = jnp.sum(jnp.exp(total - peak), keepdims=True)
    row = lax.broadcasted_iota(jnp.int32, total.shape, 0)
    mine = jnp.sum(jnp.where(row == lax.axis_index("dom"), total, 0.0), 0, keepdims=True)
    out[...] = mine - (peak + jnp.log(mass))


def normalise(parts):
    return pl.pallas_call(
        functools.partial(normalise_kernel, len(parts)),
        out_shape=jax.ShapeDtypeStruct((1, parts[0].shape[1]), jnp.float32),
        in_specs=[VMEM] * len(parts),
        out_specs=VMEM,
        cost_estimate=LIGHT,
        name="normalise",
    )(*parts)


def total_of(x, peers):
    chips = peers // 2
    side = math.isqrt(chips)
    on_chip = [(i, i ^ 1) for i in range(peers)]
    x = x + lax.ppermute(x, "dom", on_chip)
    ring = lax.axis_size("tp")
    x = x + sum(
        lax.ppermute(x, "tp", [(i, (i + hop) % ring) for i in range(ring)]) for hop in range(1, ring)
    )

    def along(i, axis):
        place = [i // (2 * side), i // 2 % side]
        place[axis] = (place[axis] + 1 - 2 * (i % 2)) % side
        return (place[0] * side + place[1]) * 2 + i % 2

    for axis in range(2):
        pairs = [(i, along(i, axis)) for i in range(peers)]
        first = lax.ppermute(x, "dom", pairs)
        parts = [x, first, lax.ppermute(first, "dom", pairs), lax.ppermute(first, "dom", on_chip)]
        x = sum(parts)
    return parts


def shards(
    cache,
    hidden,
    query_weight,
    key_projection_weight,
    value_projection_weight,
    twist_weight,
    parent_twist,
    log_ratio,
    ancestors,
):
    per_device = hidden.shape[0]
    heads = query_weight.shape[1] // HEAD_SIZE
    groups = key_projection_weight.shape[1] // HEAD_SIZE
    anchor_point = cache.shape[2]
    peers = lax.axis_size("dom")
    d = lax.axis_index("dom")
    on_chip = [(i, i ^ 1) for i in range(peers)]
    off_chip = [(i, i - 1 + 2 * (i % 2)) for i in range(1, peers - 1)]
    beside = [(i, i + 2 - 4 * (i % 2)) for i in range(peers) if 0 <= i + 2 - 4 * (i % 2) < peers]
    rows = hidden.reshape(per_device * DECODE_STEPS, -1)
    far_rows = lax.ppermute(rows, "dom", off_chip)
    mate_rows = lax.ppermute(rows, "dom", on_chip)
    count, picks, ranks = plan(ancestors, peers, per_device)
    came, skip = [], 0
    for size in PIECES:
        sent = gather(picks, cache, skip, size)
        if not came:
            sent, far_rows = lax.optimization_barrier((sent, far_rows))
        sent, picks = lax.optimization_barrier((sent, picks))
        came.append(lax.ppermute(sent, "dom", off_chip))
        skip += size
    mate_cache = lax.ppermute(cache, "dom", on_chip)
    own, mate, far, keys, values = project(
        rows, mate_rows, far_rows, query_weight, key_projection_weight, value_projection_weight,
        anchor_point,
    )
    own_part, mate_part, far_part, part, out = attend(
        ancestors, parent_twist, log_ratio, twist_weight.reshape(heads, HEAD_SIZE),
        own, mate, far, cache, peers, heads, groups,
    )
    part = jnp.sum(part, 1).reshape(4, per_device)
    index = jnp.arange(peers)[:, None]
    spread = jnp.where(
        index == d,
        part[0] + part[3],
        jnp.where(index == chip_mate(d), part[1], jnp.where(index == next_chip(d), part[2], 0.0)),
    )
    log_weights = normalise(total_of(spread, peers)).reshape(per_device)
    mate_part = lax.ppermute(mate_part, "dom", on_chip)
    far_part = lax.ppermute(far_part, "dom", on_chip)
    far_part = lax.ppermute(far_part, "dom", beside)
    owner = lax.dynamic_slice_in_dim(ancestors, d * per_device, per_device) // per_device
    owner = jnp.repeat(owner, DECODE_STEPS * heads)[:, None]
    attention = jnp.where(
        owner == d, own_part, jnp.where(owner == chip_mate(d), mate_part, far_part)
    ).reshape(per_device, DECODE_STEPS, heads * HEAD_SIZE)
    out = place_mate(ancestors, mate_cache, out)
    skip = 0
    for piece, size in zip(came, PIECES):
        out = place_far(ranks, piece, out, skip)
        skip += size
    fresh = jnp.stack([keys, values]).reshape(2, per_device, DECODE_STEPS, groups * HEAD_SIZE)

    def more(size):
        def branch(cache, picks, ranks, out):
            came = lax.ppermute(gather(picks, cache, ALWAYS, size), "dom", off_chip)
            return place_far(ranks, came, out, ALWAYS)

        return branch

    resampled_cache = lax.switch(
        jnp.maximum(count[0] - ALWAYS, 0),
        [lambda cache, picks, ranks, out: out] + [more(i + 1) for i in range(per_device - ALWAYS)],
        cache, picks, ranks, out,
    )
    return (resampled_cache, fresh, attention, log_weights)


def solution(mesh):
    return jax.shard_map(
        shards,
        mesh=mesh,
        in_specs=(
            P(None, "dom", None, "tp"),
            P("dom", None, None),
            P(None, "tp"),
            P(None, "tp"),
            P(None, "tp"),
            P("tp"),
            P("dom"),
            P("dom", None),
            P(),
        ),
        out_specs=(
            P(None, "dom", None, "tp"),
            P(None, "dom", None, "tp"),
            P("dom", None, "tp"),
            P("dom"),
        ),
        check_vma=False,
    )
```

time: 357 us -> 86.8 us (0.24)
  the two profiles are of different devices: /device:TPU:0 before, /device:TPU:70 now
where the time goes in v1:
time: 86.8 us; the launch traced here: 86.5 us
  Pallas kernels  31.8 us (37%)
  waiting for transfers between devices  25.6 us (29%)
  starting transfers between devices  19.9 us (23%)
  local copies, waits for them, and re-layouts  6.19 us (7%)
  between operations  1.64 us (2%)
  other arithmetic  1.33 us (2%)
    ppermute x2, waiting for transfers between devices, total_of(): first = lax.ppermute(x, 'dom', pairs)  13.7 us
    pallas_call x2, Pallas kernels, place(): pl.pallas_call(kernel, out_shape=pltpu.HBM(placed.shape, placed.dtype), i...  9.38 us
    pallas_call x1, Pallas kernels, project(): pl.pallas_call(functools.partial(project_kernel, heads, groups), grid=(de...  7.93 us
    pallas_call x1, Pallas kernels, attend(): pl.pallas_call(functools.partial(attend_kernel, peers, per_device, heads,...  6.46 us
    ppermute x1, starting transfers between devices, shards(): far_rows = lax.ppermute(rows, 'dom', off_chip)  5.28 us
    ppermute x2, waiting for transfers between devices, total_of(): lax.ppermute(first, 'dom', pairs)  4.74 us
    pallas_call x1, Pallas kernels, gather(): pl.pallas_call(functools.partial(gather_kernel, skip, size), out_shape=ja...  4.64 us
    unnamed x33, local copies, waits for them, and re-layouts  4.13 us
  transfers between devices with their start and end apart: 17, of which 9 were waited for; matrix products, arithmetic and copies ran while one was open for 4% of the time, Pallas kernels for 30%

profile of v1, /device:TPU:70, one launch (start us, length us, event | category | flops | bytes accessed | tf_op | source)
XLA Modules:
  0.0 86.5 jit_solution(6311712241406336502)
XLA Ops:
  0.7 1.0 %reshape.78.own = bf16[32,4096]{1,0:T(8,128)(2,1)S(1)} reshape(bf16[16,2,4096]{2,1,0:T(2,128)(2,1)} %param.21) | data formatting | bytes 524288 | tf_op jit(solution)/shard_map/reshape | solution.py:574
  1.8 5.3 %collective-permute-start.8 = (bf16[32,4096]{1,0:T(8,128)(2,1)S(1)}, bf16[32,4096]{1,0:T(8,128)(2,1)S(1)}, u32[]{:S(2)}, u32[]{:S(2)}) collective-permute-start(bf16[32,4096]{1,0:T(8,128)(2,1)S(1)} %reshape.78.own), channel_id=1, source_target_pairs={{4,8},{8,4},{12,16},{16,12},{20,24},{24,20},{28,32},{32,28},{36,40... | collective-permute-start | bytes 786440 | tf_op jit(solution)/shard_map/ppermute | solution.py:575
  7.1 1.9 %plan.1 = (s32[1]{0:T(128)}, s32[16]{0:T(128)S(1)}, s32[16]{0:T(128)S(1)}) custom-call(s32[512]{0:T(512)} %refs_0_.1, s32[4,128]{1,0:T(4,128)} %bitcast.4), custom_call_target="tpu_custom_call" | custom-call | tf_op jit(solution)/shard_map/plan/pallas_call | solution.py:94
  9.0 4.6 %gather.17 = bf16[2,8,512,256]{3,2,1,0:T(8,128)(2,1)} custom-call(s32[16]{0:T(128)S(1)} %get-tuple-element.138.picks, bf16[2,16,512,256]{3,2,1,0:T(8,128)(2,1)} %cache.3), custom_call_target="tpu_custom_call" | custom-call | tf_op jit(solution)/shard_map/gather/pallas_call | solution.py:135
  13.7 3.2 %collective-permute-start.9 = (bf16[2,8,512,256]{3,2,1,0:T(8,128)(2,1)}, bf16[2,8,512,256]{3,2,1,0:T(8,128)(2,1)}, u32[]{:S(2)}, u32[]{:S(2)}) collective-permute-start(bf16[2,8,512,256]{3,2,1,0:T(8,128)(2,1)} %gather.17), channel_id=1, source_target_pairs={{4,8},{8,4},{12,16},{16,12},{20,24},{24,20},{28,32},{32,28},{36,40... | collective-permute-start | bytes 12582920 | tf_op jit(solution)/shard_map/ppermute | solution.py:584
  17.1 1.4 %collective-permute-done.11.mate = bf16[32,4096]{1,0:T(8,128)(2,1)S(1)} collective-permute-done((bf16[32,4096]{1,0:T(8,128)(2,1)S(1)}, bf16[32,4096]{1,0:T(8,128)(2,1)S(1)}, u32[]{:S(2)}, u32[]{:S(2)}) %collective-permute-start.11) | collective-permute-done | bytes 262176 | tf_op jit(solution)/shard_map/ppermute | solution.py:576
  18.5 0.7 copy-done.8
  19.2 7.9 %project.1 = (bf16[384,128]{1,0:T(8,128)(2,1)}, bf16[384,128]{1,0:T(8,128)(2,1)}, bf16[384,128]{1,0:T(8,128)(2,1)}, bf16[32,256]{1,0:T(8,128)(2,1)}, bf16[32,256]{1,0:T(8,128)(2,1)}) custom-call(bf16[32,4096]{1,0:T(8,128)(2,1)} %copy-done.6, bf16[32,4096]{1,0:T(8,128)(2,1)} %copy-done.8, bf16[32,4096]{1,0:T(8,128)(2,1)} %copy-done.7, bf16[4096,1024]{1,0:T(8,128)(2,1)} %wq.1, ...), custom_call_target="tpu_custom_call" | custom-call | tf_op jit(solution)/shard_map/project/pallas_call | solution.py:287
  27.2 0.9 %copy-done = bf16[384,128]{1,0:T(8,128)(2,1)S(1)} copy-done((bf16[384,128]{1,0:T(8,128)(2,1)S(1)}, bf16[384,128]{1,0:T(8,128)(2,1)}, u32[]{:S(2)}) %copy-start) | copy-done | bytes 98328
  28.1 0.9 %copy-done.1 = bf16[384,128]{1,0:T(8,128)(2,1)S(1)} copy-done((bf16[384,128]{1,0:T(8,128)(2,1)S(1)}, bf16[384,128]{1,0:T(8,128)(2,1)}, u32[]{:S(2)}) %copy-start.1) | copy-done | bytes 98328
  29.0 0.9 %copy-done.2 = bf16[384,128]{1,0:T(8,128)(2,1)S(1)} copy-done((bf16[384,128]{1,0:T(8,128)(2,1)S(1)}, bf16[384,128]{1,0:T(8,128)(2,1)}, u32[]{:S(2)}) %copy-start.2) | copy-done | bytes 98328
  29.9 6.5 %attend.1 = (bf16[256,128]{1,0:T(8,128)(2,1)S(1)}, bf16[256,128]{1,0:T(8,128)(2,1)S(1)}, bf16[256,128]{1,0:T(8,128)(2,1)S(1)}, f32[64,128]{1,0:T(8,128)S(1)}, bf16[2,16,512,256]{3,2,1,0:T(8,128)(2,1)}) custom-call(s32[512]{0:T(512)S(1)} %copy-done.3, f32[16]{0:T(128)S(1)} %copy-done.5, f32[16,2]{1,0:T(8,128)S(1)} %copy.25.log_ratio, f32[8,128]{1,0:T(8,128)S(1)} %bitcast.5, ...), custom_call_target="tpu_custom_call" | custom-call | tf_op jit(solution)/shard_map/attend/pallas_call | solution.py:479
  36.6 0.5 collective-permute-start.15
  37.1 0.8 collective-permute-done.15
  38.2 3.6 %collective-permute-start.17 = (f32[32,16]{1,0:T(8,128)S(1)}, f32[32,16]{1,0:T(8,128)S(1)}, u32[]{:S(2)}, u32[]{:S(2)}) collective-permute-start(f32[32,16]{1,0:T(8,128)S(1)} %fusion), channel_id=1, source_target_pairs={{0,2},{1,3},{2,0},{3,1},{4,6},{5,7},{6,4},{7,5},{8,10},{9,11},{10,... | collective-permute-start | bytes 6152 | tf_op jit(solution)/shard_map/ppermute | solution.py:538
  41.8 1.8 %collective-permute-done.17 = f32[32,16]{1,0:T(8,128)S(1)} collective-permute-done((f32[32,16]{1,0:T(8,128)S(1)}, f32[32,16]{1,0:T(8,128)S(1)}, u32[]{:S(2)}, u32[]{:S(2)}) %collective-permute-start.17) | collective-permute-done | bytes 2080 | tf_op jit(solution)/shard_map/ppermute | solution.py:538
  43.6 1.9 %collective-permute-done.16 = f32[32,16]{1,0:T(8,128)S(1)} collective-permute-done((f32[32,16]{1,0:T(8,128)S(1)}, f32[32,16]{1,0:T(8,128)S(1)}, u32[]{:S(2)}, u32[]{:S(2)}) %collective-permute-start.16) | collective-permute-done | bytes 2080 | tf_op jit(solution)/shard_map/ppermute | solution.py:538
  45.7 4.1 %collective-permute-done.19 = f32[32,16]{1,0:T(8,128)S(1)} collective-permute-done((f32[32,16]{1,0:T(8,128)S(1)}, f32[32,16]{1,0:T(8,128)S(1)}, u32[]{:S(2)}, u32[]{:S(2)}) %collective-permute-start.19) | collective-permute-done | bytes 2080 | tf_op jit(solution)/shard_map/ppermute | solution.py:548
  49.8 1.3 %collective-permute-start.20 = (f32[32,16]{1,0:T(8,128)S(1)}, f32[32,16]{1,0:T(8,128)S(1)}, u32[]{:S(2)}, u32[]{:S(2)}) collective-permute-start(f32[32,16]{1,0:T(8,128)S(1)} %collective-permute-done.19), channel_id=1, source_target_pairs={{0,32},{4,100},{8,40},{12,108},{16,48},{20,116},{24,56},{28,124},{... | collective-permute-start | bytes 6152 | tf_op jit(solution)/shard_map/ppermute | solution.py:549
  51.2 2.4 %collective-permute-done.20 = f32[32,16]{1,0:T(8,128)S(1)} collective-permute-done((f32[32,16]{1,0:T(8,128)S(1)}, f32[32,16]{1,0:T(8,128)S(1)}, u32[]{:S(2)}, u32[]{:S(2)}) %collective-permute-start.20) | collective-permute-done | bytes 2080 | tf_op jit(solution)/shard_map/ppermute | solution.py:549
  53.7 3.0 %collective-permute-start.13 = (bf16[256,128]{1,0:T(8,128)(2,1)S(1)}, bf16[256,128]{1,0:T(8,128)(2,1)S(1)}, u32[]{:S(2)}, u32[]{:S(2)}) collective-permute-start(bf16[256,128]{1,0:T(8,128)(2,1)S(1)} %get-tuple-element.143), channel_id=1, source_target_pairs={{0,4},{4,0},{8,12},{12,8},{16,20},{20,16},{24,28},{28,24},{32,36},... | collective-permute-start | bytes 196616 | tf_op jit(solution)/shard_map/ppermute | solution.py:604
  56.7 9.6 %collective-permute-done.22.refs_1_ = f32[32,16]{1,0:T(8,128)S(1)} collective-permute-done((f32[32,16]{1,0:T(8,128)S(1)}, f32[32,16]{1,0:T(8,128)S(1)}, u32[]{:S(2)}, u32[]{:S(2)}) %collective-permute-start.22) | collective-permute-done | bytes 2080 | tf_op jit(solution)/shard_map/ppermute | solution.py:548
  67.4 0.6 collective-permute-start.12
  68.0 1.9 %collective-permute-start.14 = (bf16[256,128]{1,0:T(8,128)(2,1)S(1)}, bf16[256,128]{1,0:T(8,128)(2,1)S(1)}, u32[]{:S(2)}, u32[]{:S(2)}) collective-permute-start(bf16[256,128]{1,0:T(8,128)(2,1)S(1)} %collective-permute-done.13), channel_id=1, source_target_pairs={{0,8},{8,16},{12,4},{16,24},{20,12},{24,32},{28,20},{32,40},{36,28... | collective-permute-start | bytes 196616 | tf_op jit(solution)/shard_map/ppermute | solution.py:605
  69.9 0.7 pad_maximum_fusion
  70.6 2.3 %collective-permute-done.23.refs_2_ = f32[32,16]{1,0:T(8,128)S(1)} collective-permute-done((f32[32,16]{1,0:T(8,128)S(1)}, f32[32,16]{1,0:T(8,128)S(1)}, u32[]{:S(2)}, u32[]{:S(2)}) %collective-permute-start.23) | collective-permute-done | bytes 2080 | tf_op jit(solution)/shard_map/ppermute | solution.py:549
  73.0 0.6 copy-done.14
  73.6 1.5 %normalise.1 = f32[1,16]{1,0:T(1,128)} custom-call(f32[32,16]{1,0:T(8,128)} %copy-done.9, f32[32,16]{1,0:T(8,128)} %copy-done.12, f32[32,16]{1,0:T(8,128)} %copy-done.14, f32[32,16]{1,0:T(8,128)} %copy-done.13), custom_call_target="tpu_custom_call" | custom-call | tf_op jit(solution)/shard_map/normalise/pallas_call | solution.py:521
  75.1 1.2 %collective-permute-done.14 = bf16[256,128]{1,0:T(8,128)(2,1)S(1)} collective-permute-done((bf16[256,128]{1,0:T(8,128)(2,1)S(1)}, bf16[256,128]{1,0:T(8,128)(2,1)S(1)}, u32[]{:S(2)}, u32[]{:S(2)}) %collective-permute-start.14) | collective-permute-done | bytes 65568 | tf_op jit(solution)/shard_map/ppermute | solution.py:605
  76.4 0.7 reshape.80
  77.1 3.2 %place_mate.1.refs_2_ = bf16[2,16,512,256]{3,2,1,0:T(8,128)(2,1)} custom-call(s32[512]{0:T(512)S(1)} %copy-done.3, bf16[2,16,512,256]{3,2,1,0:T(8,128)(2,1)} %collective-permute-done.10.refs_1_, bf16[2,16,512,256]{3,2,1,0:T(8,128)(2,1)} %get-tuple-element.137.refs_2_), custom_call_target="tpu_custom_call", output_to_operand_aliasing={{}: (2, {})} | custom-call | tf_op jit(solution)/shard_map/place_mate/pallas_call | solution.py:192
  80.3 6.2 %place_far.17 = bf16[2,16,512,256]{3,2,1,0:T(8,128)(2,1)} custom-call(s32[16]{0:T(128)S(1)} %get-tuple-element.129.refs_0_, bf16[2,8,512,256]{3,2,1,0:T(8,128)(2,1)} %collective-permute-done.9.refs_1_, bf16[2,16,512,256]{3,2,1,0:T(8,128)(2,1)} %place_mate.1.refs_2_), custom_call_target="tpu_custom_call", output_to_operand_aliasing={{}: (2, {})} | custom-call | tf_op jit(solution)/shard_map/place_far/pallas_call | solution.py:192
  (63 shorter events, 1.8 us)
Async XLA Ops:
  0.6 76.4 %collective-permute-start.10 = (bf16[2,16,512,256]{3,2,1,0:T(8,128)(2,1)}, bf16[2,16,512,256]{3,2,1,0:T(8,128)(2,1)}, u32[]{:S(2)}, u32[]{:S(2)}) collective-permute-start(bf16[2,16,512,256]{3,2,1,0:T(8,128)(2,1)} %cache.3), channel_id=1, source_target_pairs={{0,4},{4,0},{8,12},{12,8},{16,20},{20,16},{24,28},{28,24},{32,36},... | collective-permute-start | bytes 25165832 | tf_op jit(solution)/shard_map/ppermute | solution.py:586
  1.8 15.1 %copy-start.6 = (bf16[32,4096]{1,0:T(8,128)(2,1)}, bf16[32,4096]{1,0:T(8,128)(2,1)S(1)}, u32[]{:S(2)}) copy-start(bf16[32,4096]{1,0:T(8,128)(2,1)S(1)} %reshape.78.own) | copy-start | bytes 786436
  1.8 11.8 %collective-permute-start.8 = (bf16[32,4096]{1,0:T(8,128)(2,1)S(1)}, bf16[32,4096]{1,0:T(8,128)(2,1)S(1)}, u32[]{:S(2)}, u32[]{:S(2)}) collective-permute-start(bf16[32,4096]{1,0:T(8,128)(2,1)S(1)} %reshape.78.own), channel_id=1, source_target_pairs={{4,8},{8,4},{12,16},{16,12},{20,24},{24,20},{28,32},{32,28},{36,40... | collective-permute-start | bytes 786440 | tf_op jit(solution)/shard_map/ppermute | solution.py:575
  9.0 8.0 %copy-start.15 = (f32[16,2]{0,1:T(2,128)S(1)}, f32[16,2]{0,1:T(2,128)}, u32[]{:S(2)}) copy-start(f32[16,2]{0,1:T(2,128)} %param.27) | copy-start | bytes 388
  13.6 4.9 %copy-start.7 = (bf16[32,4096]{1,0:T(8,128)(2,1)}, bf16[32,4096]{1,0:T(8,128)(2,1)S(1)}, u32[]{:S(2)}) copy-start(bf16[32,4096]{1,0:T(8,128)(2,1)S(1)} %collective-permute-done.8.far) | copy-start | bytes 786436
  13.7 66.6 %collective-permute-start.9 = (bf16[2,8,512,256]{3,2,1,0:T(8,128)(2,1)}, bf16[2,8,512,256]{3,2,1,0:T(8,128)(2,1)}, u32[]{:S(2)}, u32[]{:S(2)}) collective-permute-start(bf16[2,8,512,256]{3,2,1,0:T(8,128)(2,1)} %gather.17), channel_id=1, source_target_pairs={{4,8},{8,4},{12,16},{16,12},{20,24},{24,20},{28,32},{32,28},{36,40... | collective-permute-start | bytes 12582920 | tf_op jit(solution)/shard_map/ppermute | solution.py:584
  16.9 1.6 %collective-permute-start.11 = (bf16[32,4096]{1,0:T(8,128)(2,1)S(1)}, bf16[32,4096]{1,0:T(8,128)(2,1)S(1)}, u32[]{:S(2)}, u32[]{:S(2)}) collective-permute-start(bf16[32,4096]{1,0:T(8,128)(2,1)S(1)} %reshape.78.own), channel_id=1, source_target_pairs={{0,4},{4,0},{8,12},{12,8},{16,20},{20,16},{24,28},{28,24},{32,36},... | collective-permute-start | bytes 786440 | tf_op jit(solution)/shard_map/ppermute | solution.py:576
  17.1 10.1 %copy-start.3 = (s32[512]{0:T(512)S(1)}, s32[512]{0:T(512)}, u32[]{:S(2)}) copy-start(s32[512]{0:T(512)} %refs_0_.1) | copy-start | bytes 6148
  17.1 10.1 %copy-start.4 = (f32[1024]{0:T(1024)S(1)}, f32[1024]{0:T(1024)}, u32[]{:S(2)}) copy-start(f32[1024]{0:T(1024)} %param.25) | copy-start | bytes 12292
  17.1 10.1 %copy-start.5 = (f32[16]{0:T(128)S(1)}, f32[16]{0:T(128)}, u32[]{:S(2)}) copy-start(f32[16]{0:T(128)} %parent_twist.1) | copy-start | bytes 196
  18.5 0.7 copy-start.8
  27.2 0.9 %copy-start = (bf16[384,128]{1,0:T(8,128)(2,1)S(1)}, bf16[384,128]{1,0:T(8,128)(2,1)}, u32[]{:S(2)}) copy-start(bf16[384,128]{1,0:T(8,128)(2,1)} %get-tuple-element.134.own) | copy-start | bytes 294916
  28.1 0.9 %copy-start.1 = (bf16[384,128]{1,0:T(8,128)(2,1)S(1)}, bf16[384,128]{1,0:T(8,128)(2,1)}, u32[]{:S(2)}) copy-start(bf16[384,128]{1,0:T(8,128)(2,1)} %get-tuple-element.135.mate) | copy-start | bytes 294916
  29.0 0.9 %copy-start.2 = (bf16[384,128]{1,0:T(8,128)(2,1)S(1)}, bf16[384,128]{1,0:T(8,128)(2,1)}, u32[]{:S(2)}) copy-start(bf16[384,128]{1,0:T(8,128)(2,1)} %get-tuple-element.136.far) | copy-start | bytes 294916
  29.9 37.5 %copy-start.11 = (bf16[32,256]{1,0:T(8,128)(2,1)S(1)}, bf16[32,256]{1,0:T(8,128)(2,1)}, u32[]{:S(2)}) copy-start(bf16[32,256]{1,0:T(8,128)(2,1)} %get-tuple-element.139) | copy-start | bytes 49156
  29.9 37.5 %copy-start.10 = (bf16[32,256]{1,0:T(8,128)(2,1)S(1)}, bf16[32,256]{1,0:T(8,128)(2,1)}, u32[]{:S(2)}) copy-start(bf16[32,256]{1,0:T(8,128)(2,1)} %get-tuple-element.140) | copy-start | bytes 49156
  36.6 1.3 %collective-permute-start.15 = (f32[32,16]{1,0:T(8,128)S(1)}, f32[32,16]{1,0:T(8,128)S(1)}, u32[]{:S(2)}, u32[]{:S(2)}) collective-permute-start(f32[32,16]{1,0:T(8,128)S(1)} %select_select_fusion.1), channel_id=1, source_target_pairs={{0,4},{4,0},{8,12},{12,8},{16,20},{20,16},{24,28},{28,24},{32,36},... | collective-permute-start | bytes 6152 | tf_op jit(solution)/shard_map/ppermute | solution.py:535
  38.0 3.8 %collective-permute-start.18 = (f32[32,16]{1,0:T(8,128)S(1)}, f32[32,16]{1,0:T(8,128)S(1)}, u32[]{:S(2)}, u32[]{:S(2)}) collective-permute-start(f32[32,16]{1,0:T(8,128)S(1)} %fusion), channel_id=1, source_target_pairs={{0,3},{1,0},{2,1},{3,2},{4,7},{5,4},{6,5},{7,6},{8,11},{9,8},{10,9... | collective-permute-start | bytes 6152 | tf_op jit(solution)/shard_map/ppermute | solution.py:538
  38.2 5.4 %collective-permute-start.17 = (f32[32,16]{1,0:T(8,128)S(1)}, f32[32,16]{1,0:T(8,128)S(1)}, u32[]{:S(2)}, u32[]{:S(2)}) collective-permute-start(f32[32,16]{1,0:T(8,128)S(1)} %fusion), channel_id=1, source_target_pairs={{0,2},{1,3},{2,0},{3,1},{4,6},{5,7},{6,4},{7,5},{8,10},{9,11},{10,... | collective-permute-start | bytes 6152 | tf_op jit(solution)/shard_map/ppermute | solution.py:538
  41.8 3.7 %collective-permute-start.16 = (f32[32,16]{1,0:T(8,128)S(1)}, f32[32,16]{1,0:T(8,128)S(1)}, u32[]{:S(2)}, u32[]{:S(2)}) collective-permute-start(f32[32,16]{1,0:T(8,128)S(1)} %fusion), channel_id=1, source_target_pairs={{0,1},{1,2},{2,3},{3,0},{4,5},{5,6},{6,7},{7,4},{8,9},{9,10},{10,1... | collective-permute-start | bytes 6152 | tf_op jit(solution)/shard_map/ppermute | solution.py:538
  45.6 4.2 %collective-permute-start.19 = (f32[32,16]{1,0:T(8,128)S(1)}, f32[32,16]{1,0:T(8,128)S(1)}, u32[]{:S(2)}, u32[]{:S(2)}) collective-permute-start(f32[32,16]{1,0:T(8,128)S(1)} %add_add_fusion.1), channel_id=1, source_target_pairs={{0,32},{4,100},{8,40},{12,108},{16,48},{20,116},{24,56},{28,124},{... | collective-permute-start | bytes 6152 | tf_op jit(solution)/shard_map/ppermute | solution.py:548
  49.8 1.3 %collective-permute-start.21 = (f32[32,16]{1,0:T(8,128)S(1)}, f32[32,16]{1,0:T(8,128)S(1)}, u32[]{:S(2)}, u32[]{:S(2)}) collective-permute-start(f32[32,16]{1,0:T(8,128)S(1)} %collective-permute-done.19), channel_id=1, source_target_pairs={{0,4},{4,0},{8,12},{12,8},{16,20},{20,16},{24,28},{28,24},{32,36},... | collective-permute-start | bytes 6152 | tf_op jit(solution)/shard_map/ppermute | solution.py:549
  49.8 3.7 %collective-permute-start.20 = (f32[32,16]{1,0:T(8,128)S(1)}, f32[32,16]{1,0:T(8,128)S(1)}, u32[]{:S(2)}, u32[]{:S(2)}) collective-permute-start(f32[32,16]{1,0:T(8,128)S(1)} %collective-permute-done.19), channel_id=1, source_target_pairs={{0,32},{4,100},{8,40},{12,108},{16,48},{20,116},{24,56},{28,124},{... | collective-permute-start | bytes 6152 | tf_op jit(solution)/shard_map/ppermute | solution.py:549
  53.6 19.4 %copy-start.9 = (f32[32,16]{1,0:T(8,128)}, f32[32,16]{1,0:T(8,128)S(1)}, u32[]{:S(2)}) copy-start(f32[32,16]{1,0:T(8,128)S(1)} %add_add_fusion.refs_0_) | copy-start | bytes 6148
  53.6 12.7 %collective-permute-start.22 = (f32[32,16]{1,0:T(8,128)S(1)}, f32[32,16]{1,0:T(8,128)S(1)}, u32[]{:S(2)}, u32[]{:S(2)}) collective-permute-start(f32[32,16]{1,0:T(8,128)S(1)} %add_add_fusion.refs_0_), channel_id=1, source_target_pairs={{0,8},{4,28},{8,16},{12,4},{16,24},{20,12},{24,0},{28,20},{32,40},... | collective-permute-start | bytes 6152 | tf_op jit(solution)/shard_map/ppermute | solution.py:548
  53.7 14.2 %collective-permute-start.13 = (bf16[256,128]{1,0:T(8,128)(2,1)S(1)}, bf16[256,128]{1,0:T(8,128)(2,1)S(1)}, u32[]{:S(2)}, u32[]{:S(2)}) collective-permute-start(bf16[256,128]{1,0:T(8,128)(2,1)S(1)} %get-tuple-element.143), channel_id=1, source_target_pairs={{0,4},{4,0},{8,12},{12,8},{16,20},{20,16},{24,28},{28,24},{32,36},... | collective-permute-start | bytes 196616 | tf_op jit(solution)/shard_map/ppermute | solution.py:604
  66.3 6.6 %copy-start.12 = (f32[32,16]{1,0:T(8,128)}, f32[32,16]{1,0:T(8,128)S(1)}, u32[]{:S(2)}) copy-start(f32[32,16]{1,0:T(8,128)S(1)} %collective-permute-done.22.refs_1_) | copy-start | bytes 6148
  66.3 1.7 %collective-permute-start.24 = (f32[32,16]{1,0:T(8,128)S(1)}, f32[32,16]{1,0:T(8,128)S(1)}, u32[]{:S(2)}, u32[]{:S(2)}) collective-permute-start(f32[32,16]{1,0:T(8,128)S(1)} %collective-permute-done.22.refs_1_), channel_id=1, source_target_pairs={{0,4},{4,0},{8,12},{12,8},{16,20},{20,16},{24,28},{28,24},{32,36},... | collective-permute-start | bytes 6152 | tf_op jit(solution)/shard_map/ppermute | solution.py:549
  67.4 7.7 %collective-permute-start.12 = (bf16[256,128]{1,0:T(8,128)(2,1)S(1)}, bf16[256,128]{1,0:T(8,128)(2,1)S(1)}, u32[]{:S(2)}, u32[]{:S(2)}) collective-permute-start(bf16[256,128]{1,0:T(8,128)(2,1)S(1)} %get-tuple-element.142), channel_id=1, source_target_pairs={{0,4},{4,0},{8,12},{12,8},{16,20},{20,16},{24,28},{28,24},{32,36},... | collective-permute-start | bytes 196616 | tf_op jit(solution)/shard_map/ppermute | solution.py:603
  68.0 5.0 %copy-start.13 = (f32[32,16]{1,0:T(8,128)}, f32[32,16]{1,0:T(8,128)S(1)}, u32[]{:S(2)}) copy-start(f32[32,16]{1,0:T(8,128)S(1)} %collective-permute-done.24.refs_3_) | copy-start | bytes 6148
  68.0 5.0 %collective-permute-start.23 = (f32[32,16]{1,0:T(8,128)S(1)}, f32[32,16]{1,0:T(8,128)S(1)}, u32[]{:S(2)}, u32[]{:S(2)}) collective-permute-start(f32[32,16]{1,0:T(8,128)S(1)} %collective-permute-done.22.refs_1_), channel_id=1, source_target_pairs={{0,8},{4,28},{8,16},{12,4},{16,24},{20,12},{24,0},{28,20},{32,40},... | collective-permute-start | bytes 6152 | tf_op jit(solution)/shard_map/ppermute | solution.py:549
  68.0 8.3 %collective-permute-start.14 = (bf16[256,128]{1,0:T(8,128)(2,1)S(1)}, bf16[256,128]{1,0:T(8,128)(2,1)S(1)}, u32[]{:S(2)}, u32[]{:S(2)}) collective-permute-start(bf16[256,128]{1,0:T(8,128)(2,1)S(1)} %collective-permute-done.13), channel_id=1, source_target_pairs={{0,8},{8,16},{12,4},{16,24},{20,12},{24,32},{28,20},{32,40},{36,28... | collective-permute-start | bytes 196616 | tf_op jit(solution)/shard_map/ppermute | solution.py:605
  (1 other events, 0.6 us)

commit v2 on v1

v2 whole, which is shorter than its diff:
```python
import functools
import math

import jax
import jax.numpy as jnp
import numpy as np
from jax import lax
from jax.experimental import pallas as pl
from jax.experimental.pallas import tpu as pltpu
from jax.sharding import PartitionSpec as P

HEAD_SIZE = 128
DECODE_STEPS = 2
ROPE_BASE = 500000.0
PIECES = (6, 2)
ALWAYS = sum(PIECES)
AT_ONCE = 4

SMEM = pl.BlockSpec(memory_space=pltpu.SMEM)
VMEM = pl.BlockSpec(memory_space=pltpu.VMEM)
ANY = pl.BlockSpec(memory_space=pl.ANY)
HBM = pl.BlockSpec(memory_space=pltpu.HBM)
SMALL = pltpu.CompilerParams(vmem_limit_bytes=2 * 2**20)
LIGHT = pl.CostEstimate(flops=0, bytes_accessed=0, transcendentals=0)


def chip_mate(d):
    return d + 1 - 2 * (d % 2)


def next_chip(d):
    return d - 1 + 2 * (d % 2)


def rope_tables(rows, anchor_point):
    half = HEAD_SIZE // 2
    frequency = np.exp(
        np.arange(half, dtype=np.float32) * np.float32(-2.0 * math.log(ROPE_BASE) / HEAD_SIZE)
    ).astype(np.float32)
    positions = (anchor_point + np.arange(rows) % DECODE_STEPS).astype(np.float32)
    angles = (positions[:, None] * frequency[None, :]).astype(np.float32)
    cosine = np.cos(angles).astype(np.float32)
    sine = np.sin(angles).astype(np.float32)
    return np.concatenate([cosine, cosine], 1), np.concatenate([-sine, sine], 1)


def bit_count(mask):
    mask = mask - ((mask >> 1) & 0x55555555)
    mask = (mask & 0x33333333) + ((mask >> 2) & 0x33333333)
    mask = (mask + (mask >> 4)) & 0x0F0F0F0F
    return (mask * 0x01010101) >> 24


def plan_kernel(peers, per_device, ancestors, grid, count, picks, ranks):
    d = lax.axis_index("dom")
    shape = grid.shape
    flat = lax.broadcasted_iota(jnp.int32, shape, 0) * shape[1] + lax.broadcasted_iota(
        jnp.int32, shape, 1
    )
    home = flat // per_device
    offset = grid[...] - next_chip(home) * per_device
    inside = (offset >= 0) & (offset < per_device)
    bits = jnp.where(inside, jnp.int32(1) << (offset & (per_device - 1)), 0)
    shift = 1
    while shift < per_device:
        bits = bits | pltpu.roll(bits, shape[1] - shift, 1)
        shift *= 2
    most = jnp.where(flat % per_device == 0, bit_count(bits), 0)
    count[0] = jnp.max(most.astype(jnp.float32)).astype(jnp.int32)

    def needed(home, owner):
        mask = jnp.int32(0)
        for k in range(per_device):
            offset = ancestors[home * per_device + k] - owner * per_device
            inside = (offset >= 0) & (offset < per_device)
            mask = mask | jnp.where(inside, jnp.int32(1) << (offset & (per_device - 1)), 0)
        return mask

    there = next_chip(d)
    mask = needed(jnp.clip(there, 0, peers - 1), d)
    position = jnp.int32(0)
    for j in range(per_device):
        picks[j] = 0
    for j in range(per_device):
        picks[position] = j
        position = position + ((mask >> j) & 1)
    mask = needed(d, there)
    for k in range(per_device):
        offset = ancestors[d * per_device + k] - there * per_device
        inside = (offset >= 0) & (offset < per_device)
        below = (jnp.int32(1) << (offset & (per_device - 1))) - 1
        ranks[k] = jnp.where(inside, bit_count(mask & below), -1)


def plan(ancestors, peers, per_device):
    return pl.pallas_call(
        functools.partial(plan_kernel, peers, per_device),
        out_shape=(
            jax.ShapeDtypeStruct((1,), jnp.int32),
            jax.ShapeDtypeStruct((per_device,), jnp.int32),
            jax.ShapeDtypeStruct((per_device,), jnp.int32),
        ),
        in_specs=[SMEM, VMEM],
        out_specs=(SMEM, SMEM, SMEM),
        cost_estimate=LIGHT,
        name="plan",
    )(ancestors, ancestors.reshape(-1, 128))


def gather_kernel(skip, size, picks, cache, sent, sems):
    def load(i, c):
        return pltpu.make_async_copy(cache.at[c, picks[skip + i]], sent.at[c, i], sems.at[c, i])

    def each(act):
        def body(i, carry):
            for c in range(2):
                act(load(i, c))
            return carry

        lax.fori_loop(0, size, body, 0)

    each(lambda copy: copy.start())
    each(lambda copy: copy.wait())


def gather(picks, cache, skip, size):
    shape = (2, size, *cache.shape[2:])
    return pl.pallas_call(
        functools.partial(gather_kernel, skip, size),
        out_shape=pltpu.VMEM(shape, cache.dtype),
        in_specs=[SMEM, HBM],
        out_specs=VMEM,
        scratch_shapes=[pltpu.SemaphoreType.DMA((2, size))],
        compiler_params=pltpu.CompilerParams(vmem_limit_bytes=12 * 2**20),
        cost_estimate=LIGHT,
        name="gather",
    )(picks, cache)


def place_kernel(per_device, find, tables, *refs):
    numbers, refs = refs[:tables], refs[tables:]
    *sources, _, out, held, loads, stores = refs
    d = lax.axis_index("dom")

    def each(act):
        def body(k, carry):
            for source, (there, at) in zip(sources, find(numbers, d, k)):

                @pl.when(there)
                def _():
                    for c in range(2):
                        act(source, at, k, c)

            return carry

        lax.fori_loop(0, per_device, body, 0)

    def load(source, at, k, c):
        return pltpu.make_async_copy(source.at[c, at], held.at[c, k], loads.at[c, k])

    def store(k, c):
        return pltpu.make_async_copy(held.at[c, k], out.at[c, k], stores.at[c, k])

    def forward(source, at, k, c):
        load(source, at, k, c).wait()
        store(k, c).start()

    each(lambda source, at, k, c: load(source, at, k, c).start())
    each(forward)
    each(lambda source, at, k, c: store(k, c).wait())


def place(find, numbers, sources, placed, name):
    per_device = placed.shape[1]
    operands = [*numbers, *sources, placed]
    return pl.pallas_call(
        functools.partial(place_kernel, per_device, find, len(numbers)),
        out_shape=pltpu.HBM(placed.shape, placed.dtype),
        in_specs=[SMEM] * len(numbers) + [ANY] * len(sources) + [HBM],
        out_specs=HBM,
        scratch_shapes=[
            pltpu.VMEM(placed.shape, placed.dtype),
            pltpu.SemaphoreType.DMA((2, per_device)),
            pltpu.SemaphoreType.DMA((2, per_device)),
        ],
        input_output_aliases={len(operands) - 1: 0},
        compiler_params=pltpu.CompilerParams(vmem_limit_bytes=12 * 2**20),
        cost_estimate=LIGHT,
        name=name,
    )(*operands)


def place_first(ancestors, ranks, mate, came, placed):
    per_device, size = placed.shape[1], came.shape[1]

    def find(numbers, d, k):
        ancestors, ranks = numbers
        offset = ancestors[d * per_device + k] - chip_mate(d) * per_device
        yield (offset >= 0) & (offset < per_device), offset
        yield (ranks[k] >= 0) & (ranks[k] < size), ranks[k]

    return place(find, [ancestors, ranks], [mate, came], placed, "place_first")


def place_more(ranks, came, placed, skip):
    size = came.shape[1]

    def find(numbers, d, k):
        rank = numbers[0][k] - skip
        yield (rank >= 0) & (rank < size), rank

    return place(find, [ranks], [came], placed, "place_more")


def serve_kernel(
    peers, per_device, heads, groups,
    ancestors, parent_twist, log_ratio, twist_weight, own, mate, far, cosine, sine, wq, wk, wv, cache,
    keys, values, out_own, out_others, part, placed,
    held, weights_q, weights_k, weights_v, total, turned, tokens, fresh, results,
    lists, slots, owners, loads, stores, streams,
):
    d = lax.axis_index("dom")
    first_lane = (lax.axis_index("tp") == 0).astype(jnp.float32)
    tile = DECODE_STEPS * heads
    queries = per_device * tile
    small = per_device * DECODE_STEPS
    homes = (d, chip_mate(d), next_chip(d))
    width_q, width_k = heads * HEAD_SIZE, groups * HEAD_SIZE
    chunks = streams.shape[1]
    depth = wq.shape[0] // chunks

    def stream(i, k):
        rows = pl.ds(pl.multiple_of(k * depth, depth), depth)
        source, target = ((wq, weights_q), (wk, weights_k), (wv, weights_v))[i]
        return pltpu.make_async_copy(source.at[rows, :], target.at[rows, :], streams.at[i, k])

    def begin(k, carry):
        for i in range(3):
            stream(i, k).start()
        return carry

    lax.fori_loop(0, chunks, begin, 0)

    def load(j, c):
        return pltpu.make_async_copy(cache.at[c, j], held.at[c, j], loads.at[c, j])

    def clear(j, carry):
        lists[j] = -1
        return carry

    lax.fori_loop(0, per_device, clear, 0)
    for h, home in enumerate(homes):
        there = (home >= 0) & (home < peers)
        start = jnp.clip(home, 0, peers - 1) * per_device

        def enlist(k, carry):
            offset = ancestors[start + k] - d * per_device

            @pl.when(there & (offset >= 0) & (offset < per_device))
            def _():
                slot = h * per_device + k
                lists[per_device + slot] = lists[offset]
                lists[offset] = slot

            return carry

        lax.fori_loop(0, per_device, enlist, 0)

    def flatten(j, count):
        def step(state):
            slot, count = state
            slots[count] = slot
            owners[count] = j
            return lists[per_device + slot], count + 1

        return lax.while_loop(lambda state: state[0] >= 0, step, (lists[j], count))[1]

    count = lax.fori_loop(0, per_device, flatten, jnp.int32(0))
    for extra in range(AT_ONCE - 1):

        @pl.when(count > 0)
        def _():
            slots[count + extra] = slots[count - 1]
            owners[count + extra] = owners[count - 1]

    part[...] = jnp.zeros_like(part)
    part[3 * per_device :, :DECODE_STEPS] = log_ratio[...] * first_lane
    results[...] = jnp.zeros_like(results)
    total[...] = jnp.zeros_like(total)
    per_chunk = per_device // chunks

    def project(k, carry):
        for i in range(3):
            stream(i, k).wait()
        for j in range(per_chunk):
            for c in range(2):
                load(k * per_chunk + j, c).start()
        at = pl.ds(pl.multiple_of(k * depth, depth), depth)
        rows = jnp.concatenate([own[:, at], mate[:, at], far[:, at]], 0)
        lanes = 0
        for weight, width in ((weights_q, width_q), (weights_k, width_k), (weights_v, width_k)):
            total[:, lanes : lanes + width] += jnp.dot(
                rows, weight[at, :], preferred_element_type=jnp.float32
            )
            lanes += width
        return carry

    lax.fori_loop(0, chunks, project, 0)

    def turn(x):
        return x * cosine[...] + pltpu.roll(x, HEAD_SIZE // 2, 1) * sine[...]

    block = 2 * groups * small
    for h in range(3):
        mine = slice(h * small, (h + 1) * small)
        for i in range(heads):
            turned[:, i, :] = turn(total[mine, i * HEAD_SIZE : (i + 1) * HEAD_SIZE])
        tokens[h * queries : (h + 1) * queries, :] = (
            turned[...].reshape(queries, HEAD_SIZE).astype(tokens.dtype)
        )
        for g in range(groups):
            lanes = slice(g * HEAD_SIZE, (g + 1) * HEAD_SIZE)
            at = width_q + g * HEAD_SIZE
            key = turn(total[mine, at : at + HEAD_SIZE]).astype(keys.dtype)
            at = at + width_k
            value = total[mine, at : at + HEAD_SIZE].astype(values.dtype)
            at = h * block + g * small
            fresh[at : at + small, :] = key.astype(jnp.float32)
            at = at + groups * small
            fresh[at : at + small, :] = value.astype(jnp.float32)
            if h == 0:
                keys[:, lanes] = key
                values[:, lanes] = value

    row = lax.broadcasted_iota(jnp.int32, (tile, 1), 0)
    lower = (row % heads) < heads // groups
    later = row >= heads
    lane = lax.broadcasted_iota(jnp.int32, (1, HEAD_SIZE), 1)
    scale = 1.0 / math.sqrt(HEAD_SIZE)
    twist = jnp.concatenate([jnp.zeros_like(twist_weight), twist_weight[...]], 0)

    def by_group(at):
        pair = [fresh[pl.ds(at + g * small, 1), :] for g in range(groups)]
        return jnp.where(lower, pair[0], pair[1])

    def scores_of(j, slot):
        query = tokens[pl.ds(pl.multiple_of(slot * tile, tile), tile), :]
        none = jnp.zeros_like(query)
        wide = jnp.concatenate([jnp.where(lower, query, none), jnp.where(lower, none, query)], 1)
        scores = (
            lax.dot_general(
                wide, held[0, j], (((1,), (1,)), ((), ())), preferred_element_type=jnp.float32
            )
            * scale
        )
        return query.astype(jnp.float32), scores

    def weights_of(scores):
        maxima = jnp.max(scores, 1, keepdims=True)
        return maxima, jnp.exp(scores - maxima)

    def finish(j, slot, query, maxima, totals, both):
        weighted = jnp.where(lower, both[:, :HEAD_SIZE], both[:, HEAD_SIZE:])
        at = (slot // per_device) * block + (slot % per_device) * DECODE_STEPS
        new = [
            jnp.sum(query * by_group(at + u), 1, keepdims=True) * scale
            for u in range(DECODE_STEPS)
        ]
        new[1] = jnp.where(later, new[1], -jnp.inf)
        peak = jnp.maximum(maxima, jnp.maximum(new[0], new[1]))
        carried = jnp.exp(maxima - peak)
        numerator = carried * weighted
        denominator = carried * totals
        for u in range(DECODE_STEPS):
            share = jnp.exp(new[u] - peak)
            numerator = numerator + share * by_group(at + groups * small + u)
            denominator = denominator + share
        outputs = numerator / denominator
        results[pl.ds(pl.multiple_of(slot * tile, tile), tile), :] = outputs.astype(jnp.bfloat16)
        twisted = jnp.sum(outputs * twist, 0, keepdims=True)
        less = jnp.where(lane == 0, parent_twist[j] * first_lane, 0.0)
        part[pl.ds(slot, 1), :] = twisted - less

    def store(k, j, c):
        return pltpu.make_async_copy(held.at[c, j], placed.at[c, k], stores.at[c, k])

    def arrive(j, carry):
        for c in range(2):
            load(j, c).wait()

        def step(slot):
            @pl.when(slot < per_device)
            def _():
                for c in range(2):
                    store(slot, j, c).start()

            return lists[per_device + slot]

        lax.while_loop(lambda slot: slot >= 0, step, lists[j])
        return carry

    def serve(step, loaded):
        at = step * AT_ONCE
        last = owners[at + AT_ONCE - 1] + 1
        lax.fori_loop(loaded, last, arrive, 0)
        jobs = [(owners[at + i], slots[at + i]) for i in range(AT_ONCE)]
        scored = [scores_of(*job) for job in jobs]
        weights = [weights_of(scores) for _, scores in scored]
        totals = [jnp.sum(expo, 1, keepdims=True) for _, expo in weights]
        both = [
            jnp.dot(expo.astype(jnp.bfloat16), held[1, job[0]], preferred_element_type=jnp.float32)
            for job, (_, expo) in zip(jobs, weights)
        ]
        for i, job in enumerate(jobs):
            finish(*job, scored[i][0], weights[i][0], totals[i], both[i])
        return last

    loaded = lax.fori_loop(0, (count + AT_ONCE - 1) // AT_ONCE, serve, jnp.int32(0))
    lax.fori_loop(loaded, per_device, arrive, 0)
    out_own[...] = results[:queries, :]
    out_others[...] = results[queries:, :]

    def settle(k, carry):
        offset = ancestors[d * per_device + k] - d * per_device

        @pl.when((offset >= 0) & (offset < per_device))
        def _():
            for c in range(2):
                store(k, offset, c).wait()

        return carry

    lax.fori_loop(0, per_device, settle, 0)


def serve(ancestors, parent_twist, log_ratio, twist_weight, own, mate, far, wq, wk, wv, cache, peers):
    per_device, anchor_point = cache.shape[1:3]
    heads, groups = wq.shape[1] // HEAD_SIZE, wk.shape[1] // HEAD_SIZE
    tile = DECODE_STEPS * heads
    queries = per_device * tile
    small = per_device * DECODE_STEPS
    cosine, sine = rope_tables(small, anchor_point)
    columns = wq.shape[1] + wk.shape[1] + wv.shape[1]
    chunks = 8
    return pl.pallas_call(
        functools.partial(serve_kernel, peers, per_device, heads, groups),
        out_shape=(
            jax.ShapeDtypeStruct((small, groups * HEAD_SIZE), jnp.bfloat16),
            jax.ShapeDtypeStruct((small, groups * HEAD_SIZE), jnp.bfloat16),
            jax.ShapeDtypeStruct((queries, HEAD_SIZE), jnp.bfloat16),
            jax.ShapeDtypeStruct((2 * queries, HEAD_SIZE), jnp.bfloat16),
            jax.ShapeDtypeStruct((4 * per_device, HEAD_SIZE), jnp.float32),
            pltpu.HBM(cache.shape, cache.dtype),
        ),
        in_specs=[SMEM, SMEM] + [VMEM] * 7 + [HBM] * 4,
        out_specs=(VMEM, VMEM, VMEM, VMEM, VMEM, HBM),
        scratch_shapes=[
            pltpu.VMEM(cache.shape, cache.dtype),
            pltpu.VMEM(wq.shape, wq.dtype),
            pltpu.VMEM(wk.shape, wk.dtype),
            pltpu.VMEM(wv.shape, wv.dtype),
            pltpu.VMEM((3 * small, columns), jnp.float32),
            pltpu.VMEM((small, heads, HEAD_SIZE), jnp.float32),
            pltpu.VMEM((3 * queries, HEAD_SIZE), jnp.bfloat16),
            pltpu.VMEM((3 * 2 * groups * small, HEAD_SIZE), jnp.float32),
            pltpu.VMEM((3 * queries, HEAD_SIZE), jnp.bfloat16),
            pltpu.SMEM((4 * per_device,), jnp.int32),
            pltpu.SMEM((3 * per_device + AT_ONCE,), jnp.int32),
            pltpu.SMEM((3 * per_device + AT_ONCE,), jnp.int32),
            pltpu.SemaphoreType.DMA((2, per_device)),
            pltpu.SemaphoreType.DMA((2, per_device)),
            pltpu.SemaphoreType.DMA((3, chunks)),
        ],
        compiler_params=pltpu.CompilerParams(vmem_limit_bytes=59 * 2**20),
        cost_estimate=LIGHT,
        name="serve",
    )(ancestors, parent_twist, log_ratio, twist_weight, own, mate, far, cosine, sine, wq, wk, wv, cache)


def normalise_kernel(terms, *refs):
    *parts, out = refs
    del terms
    total = parts[0][...]
    for part in parts[1:]:
        total = total + part[...]
    peak = jnp.max(total, keepdims=True)
    mass = jnp.sum(jnp.exp(total - peak), keepdims=True)
    row = lax.broadcasted_iota(jnp.int32, total.shape, 0)
    mine = jnp.sum(jnp.where(row == lax.axis_index("dom"), total, 0.0), 0, keepdims=True)
    out[...] = mine - (peak + jnp.log(mass))


def normalise(parts):
    return pl.pallas_call(
        functools.partial(normalise_kernel, len(parts)),
        out_shape=jax.ShapeDtypeStruct((1, parts[0].shape[1]), jnp.float32),
        in_specs=[VMEM] * len(parts),
        out_specs=VMEM,
        compiler_params=SMALL,
        cost_estimate=LIGHT,
        name="normalise",
    )(*parts)


def total_but_y(x, peers):
    side = math.isqrt(peers // 2)
    on_chip = [(i, i ^ 1) for i in range(peers)]
    x = x + lax.ppermute(x, "dom", on_chip)
    ring, hop = lax.axis_size("tp"), 1
    while hop < ring:
        x = x + lax.ppermute(x, "tp", [(i, i ^ hop) for i in range(ring)])
        hop *= 2
    step = 2 * side
    pairs = [(i, (i + step * (1 - 2 * (i % 2))) % peers) for i in range(peers)]
    first = lax.ppermute(x, "dom", pairs)
    return x + first + lax.ppermute(first, "dom", pairs) + lax.ppermute(first, "dom", on_chip)


def parts_along_y(x, peers):
    step = 2 * math.isqrt(peers // 2)
    parts = [x]
    for hop in range(2, step, 2):
        pairs = [(i, i // step * step + (i + hop) % step) for i in range(peers)]
        parts.append(lax.ppermute(x, "dom", pairs))
    return parts


def shards(
    cache,
    hidden,
    query_weight,
    key_projection_weight,
    value_projection_weight,
    twist_weight,
    parent_twist,
    log_ratio,
    ancestors,
):
    per_device = hidden.shape[0]
    heads = query_weight.shape[1] // HEAD_SIZE
    groups = key_projection_weight.shape[1] // HEAD_SIZE
    peers = lax.axis_size("dom")
    d = lax.axis_index("dom")
    on_chip = [(i, i ^ 1) for i in range(peers)]
    off_chip = [(i, i - 1 + 2 * (i % 2)) for i in range(1, peers - 1)]
    beside = [(i, i + 2 - 4 * (i % 2)) for i in range(peers) if 0 <= i + 2 - 4 * (i % 2) < peers]
    rows = hidden.reshape(per_device * DECODE_STEPS, -1)
    far_rows = lax.ppermute(rows, "dom", off_chip)
    mate_rows = lax.ppermute(rows, "dom", on_chip)
    count, picks, ranks = plan(ancestors, peers, per_device)
    came, skip = [], 0
    for size in PIECES:
        sent = gather(picks, cache, skip, size)
        if not came:
            sent, far_rows = lax.optimization_barrier((sent, far_rows))
        sent, picks = lax.optimization_barrier((sent, picks))
        came.append(lax.ppermute(sent, "dom", off_chip))
        skip += size
    late_cache, far_rows, mate_rows = lax.optimization_barrier((cache, far_rows, mate_rows))
    mate_cache = lax.ppermute(late_cache, "dom", on_chip)
    keys, values, own_part, others_part, part, out = serve(
        ancestors, parent_twist, log_ratio, twist_weight.reshape(heads, HEAD_SIZE),
        rows, mate_rows, far_rows, query_weight, key_projection_weight, value_projection_weight,
        cache, peers,
    )
    part = jnp.sum(part, 1).reshape(4, per_device)
    index = jnp.arange(peers)[:, None]
    spread = jnp.where(
        index == d,
        part[0] + part[3],
        jnp.where(index == chip_mate(d), part[1], jnp.where(index == next_chip(d), part[2], 0.0)),
    )
    spread = total_but_y(spread, peers)
    mate_part, far_part = jnp.split(lax.ppermute(others_part, "dom", on_chip), 2)
    far_part = lax.ppermute(far_part, "dom", beside)
    owner = lax.dynamic_slice_in_dim(ancestors, d * per_device, per_device) // per_device
    owner = jnp.repeat(owner, DECODE_STEPS * heads)[:, None]
    attention = jnp.where(
        owner == d, own_part, jnp.where(owner == chip_mate(d), mate_part, far_part)
    ).reshape(per_device, DECODE_STEPS, heads * HEAD_SIZE)
    out = place_first(ancestors, ranks, mate_cache, came[0], out)
    spread, out = lax.optimization_barrier((spread, out))
    log_weights = normalise(parts_along_y(spread, peers)).reshape(per_device)
    fresh = jnp.stack([keys, values]).reshape(2, per_device, DECODE_STEPS, groups * HEAD_SIZE)

    def more(size):
        def branch(cache, picks, ranks, out):
            came = lax.ppermute(gather(picks, cache, ALWAYS, size), "dom", off_chip)
            return place_more(ranks, came, out, ALWAYS)

        return branch

    out = lax.switch(
        jnp.maximum(count[0] - ALWAYS, 0),
        [lambda cache, picks, ranks, out: out] + [more(i + 1) for i in range(per_device - ALWAYS)],
        cache, picks, ranks, out,
    )
    skip = PIECES[0]
    for piece in came[1:]:
        out = place_more(ranks, piece, out, skip)
        skip += piece.shape[1]
    return (out, fresh, attention, log_weights)


def solution(mesh):
    return jax.shard_map(
        shards,
        mesh=mesh,
        in_specs=(
            P(None, "dom", None, "tp"),
            P("dom", None, None),
            P(None, "tp"),
            P(None, "tp"),
            P(None, "tp"),
            P("tp"),
            P("dom"),
            P("dom", None),
            P(),
        ),
        out_specs=(
            P(None, "dom", None, "tp"),
            P(None, "dom", None, "tp"),
            P("dom", None, "tp"),
            P("dom"),
        ),
        check_vma=False,
    )
```

time: 86.8 us -> 72.1 us (0.83)
  the two profiles are of different devices: /device:TPU:70 before, /device:TPU:0 now
where the time goes in v2:
time: 72.1 us; the launch traced here: 71.9 us
  starting transfers between devices  35.6 us (49%)
  Pallas kernels  25.6 us (36%)
  waiting for transfers between devices  4.32 us (6%)
  local copies, waits for them, and re-layouts  2.77 us (4%)
  other arithmetic  2.09 us (3%)
  between operations  1.54 us (2%)
    pallas_call x1, Pallas kernels, serve(): pl.pallas_call(functools.partial(serve_kernel, peers, per_device, heads,...  11.4 us
    ppermute x3, starting transfers between devices, parts_along_y(): parts.append(lax.ppermute(x, 'dom', pairs))  8.42 us
    pallas_call x2, Pallas kernels, place(): pl.pallas_call(functools.partial(place_kernel, per_device, find, len(numb...  6.3 us
    ppermute x1, starting transfers between devices, total_but_y(): first = lax.ppermute(x, 'dom', pairs)  5.9 us
    ppermute x2, starting transfers between devices, total_but_y(): x = x + lax.ppermute(x, 'tp', [(i, i ^ hop) for i in range(ring)])  5.66 us
    pallas_call x2, Pallas kernels, gather(): pl.pallas_call(functools.partial(gather_kernel, skip, size), out_shape=pl...  5.24 us
    ppermute x2, starting transfers between devices, shards(): came.append(lax.ppermute(sent, 'dom', off_chip))  3.98 us
    ppermute x1, waiting for transfers between devices, total_but_y(): lax.ppermute(first, 'dom', pairs)  2.52 us
  transfers between devices with their start and end apart: 16, of which 3 were waited for; matrix products, arithmetic and copies ran while one was open for 5% of the time, Pallas kernels for 35%

profile of v2, /device:TPU:0, one launch (start us, length us, event | category | flops | bytes accessed | tf_op | source)
XLA Modules:
  0.0 71.9 jit_solution(14158791383923694811)
XLA Ops:
  0.6 1.0 %reshape.78.own = bf16[32,4096]{1,0:T(8,128)(2,1)S(1)} reshape(bf16[16,2,4096]{2,1,0:T(2,128)(2,1)} %param.21) | data formatting | bytes 524288 | tf_op jit(solution)/shard_map/reshape | solution.py:547
  1.7 1.4 %collective-permute-start.8 = (bf16[32,4096]{1,0:T(8,128)(2,1)S(1)}, bf16[32,4096]{1,0:T(8,128)(2,1)}, u32[]{:S(2)}, u32[]{:S(2)}) collective-permute-start(bf16[32,4096]{1,0:T(8,128)(2,1)S(1)} %reshape.78.own), channel_id=1, source_target_pairs={{4,8},{8,4},{12,16},{16,12},{20,24},{24,20},{28,32},{32,28},{36,40... | collective-permute-start | bytes 786440 | tf_op jit(solution)/shard_map/ppermute | solution.py:548
  3.1 2.4 %collective-permute-start.10 = (bf16[32,4096]{1,0:T(8,128)(2,1)S(1)}, bf16[32,4096]{1,0:T(8,128)(2,1)}, u32[]{:S(2)}, u32[]{:S(2)}) collective-permute-start(bf16[32,4096]{1,0:T(8,128)(2,1)S(1)} %reshape.78.own), channel_id=1, source_target_pairs={{0,4},{4,0},{8,12},{12,8},{16,20},{20,16},{24,28},{28,24},{32,36},... | collective-permute-start | bytes 786440 | tf_op jit(solution)/shard_map/ppermute | solution.py:549
  5.5 1.9 %plan.1 = (s32[1]{0:T(128)}, s32[16]{0:T(128)S(1)}, s32[16]{0:T(128)S(1)}) custom-call(s32[512]{0:T(512)} %refs_0_.1, s32[4,128]{1,0:T(4,128)} %bitcast.4), custom_call_target="tpu_custom_call" | custom-call | tf_op jit(solution)/shard_map/plan/pallas_call | solution.py:96
  7.4 2.5 %gather.18 = bf16[2,6,512,256]{3,2,1,0:T(8,128)(2,1)S(1)} custom-call(s32[16]{0:T(128)S(1)} %get-tuple-element.145.picks, bf16[2,16,512,256]{3,2,1,0:T(8,128)(2,1)} %cache.5), custom_call_target="tpu_custom_call" | custom-call | tf_op jit(solution)/shard_map/gather/pallas_call | solution.py:128
  9.9 0.1 collective-permute-start.17
  10.0 2.3 %collective-permute-start.18 = (bf16[2,6,512,256]{3,2,1,0:T(8,128)(2,1)S(1)}, bf16[2,6,512,256]{3,2,1,0:T(8,128)(2,1)}, u32[]{:S(2)}, u32[]{:S(2)}) collective-permute-start(bf16[2,6,512,256]{3,2,1,0:T(8,128)(2,1)S(1)} %gather.18), channel_id=1, source_target_pairs={{4,8},{8,4},{12,16},{16,12},{20,24},{24,20},{28,32},{32,28},{36,40... | collective-permute-start | bytes 9437192 | tf_op jit(solution)/shard_map/ppermute | solution.py:557
  12.3 0.7 copy.25.log_ratio
  13.0 11.4 %serve.1 = (bf16[32,256]{1,0:T(8,128)(2,1)}, bf16[32,256]{1,0:T(8,128)(2,1)}, bf16[256,128]{1,0:T(8,128)(2,1)}, bf16[512,128]{1,0:T(8,128)(2,1)}, f32[64,128]{1,0:T(8,128)}, /*index=5*/bf16[2,16,512,256]{3,2,1,0:T(8,128)(2,1)}) custom-call(s32[512]{0:T(512)} %refs_0_.1, f32[16]{0:T(128)} %parent_twist.1, f32[16,2]{1,0:T(8,128)} %copy.25.log_ratio, ...), custom_call_target="tpu_custom_call" | custom-call | tf_op jit(solution)/shard_map/serve/pallas_call | solution.py:445
  24.4 0.9 %reduce_sum.9 = f32[64]{0:T(128)S(1)} reduce(f32[64,128]{1,0:T(8,128)} %get-tuple-element.140, f32[]{:T(128)} %constant.49.clone.1), dimensions={1}, to_apply=%region_0.0 | reduce | flops 8128 | bytes 33028 | tf_op jit(solution)/shard_map/reduce_sum | solution.py:566
  25.4 1.9 %collective-permute-start.11 = (f32[32,16]{1,0:T(8,128)S(1)}, f32[32,16]{1,0:T(8,128)S(1)}, u32[]{:S(2)}, u32[]{:S(2)}) collective-permute-start(f32[32,16]{1,0:T(8,128)S(1)} %select_select_fusion), channel_id=1, source_target_pairs={{0,4},{4,0},{8,12},{12,8},{16,20},{20,16},{24,28},{28,24},{32,36},... | collective-permute-start | bytes 6152 | tf_op jit(solution)/shard_map/ppermute | solution.py:508
  27.3 0.8 %collective-permute-done.11 = f32[32,16]{1,0:T(8,128)S(1)} collective-permute-done((f32[32,16]{1,0:T(8,128)S(1)}, f32[32,16]{1,0:T(8,128)S(1)}, u32[]{:S(2)}, u32[]{:S(2)}) %collective-permute-start.11) | collective-permute-done | bytes 2080 | tf_op jit(solution)/shard_map/ppermute | solution.py:508
  28.3 2.0 %collective-permute-start.12 = (f32[32,16]{1,0:T(8,128)S(1)}, f32[32,16]{1,0:T(8,128)S(1)}, u32[]{:S(2)}, u32[]{:S(2)}) collective-permute-start(f32[32,16]{1,0:T(8,128)S(1)} %fusion.1), channel_id=1, source_target_pairs={{0,1},{1,0},{2,3},{3,2},{4,5},{5,4},{6,7},{7,6},{8,9},{9,8},{10,11... | collective-permute-start | bytes 6152 | tf_op jit(solution)/shard_map/ppermute | solution.py:511
  30.3 2.8 %gather.19 = bf16[2,2,512,256]{3,2,1,0:T(8,128)(2,1)} custom-call(s32[16]{0:T(128)S(1)} %get-tuple-element.145.picks, bf16[2,16,512,256]{3,2,1,0:T(8,128)(2,1)} %cache.5), custom_call_target="tpu_custom_call" | custom-call | tf_op jit(solution)/shard_map/gather/pallas_call | solution.py:128
  33.0 1.7 %collective-permute-start.9 = (bf16[2,2,512,256]{3,2,1,0:T(8,128)(2,1)}, bf16[2,2,512,256]{3,2,1,0:T(8,128)(2,1)}, u32[]{:S(2)}, u32[]{:S(2)}) collective-permute-start(bf16[2,2,512,256]{3,2,1,0:T(8,128)(2,1)} %gather.19), channel_id=1, source_target_pairs={{4,8},{8,4},{12,16},{16,12},{20,24},{24,20},{28,32},{32,28},{36,40... | collective-permute-start | bytes 3145736 | tf_op jit(solution)/shard_map/ppermute | solution.py:557
  34.8 3.7 %collective-permute-start.13 = (f32[32,16]{1,0:T(8,128)S(1)}, f32[32,16]{1,0:T(8,128)S(1)}, u32[]{:S(2)}, u32[]{:S(2)}) collective-permute-start(f32[32,16]{1,0:T(8,128)S(1)} %fusion.2), channel_id=1, source_target_pairs={{0,2},{1,3},{2,0},{3,1},{4,6},{5,7},{6,4},{7,5},{8,10},{9,11},{10,... | collective-permute-start | bytes 6152 | tf_op jit(solution)/shard_map/ppermute | solution.py:511
  38.6 2.0 %collective-permute-start.19 = (bf16[512,128]{1,0:T(8,128)(2,1)}, bf16[512,128]{1,0:T(8,128)(2,1)S(1)}, u32[]{:S(2)}, u32[]{:S(2)}) collective-permute-start(bf16[512,128]{1,0:T(8,128)(2,1)} %get-tuple-element.149), channel_id=1, source_target_pairs={{0,4},{4,0},{8,12},{12,8},{16,20},{20,16},{24,28},{28,24},{32,36},... | collective-permute-start | bytes 393224 | tf_op jit(solution)/shard_map/ppermute | solution.py:574
  40.5 5.9 %collective-permute-start.14 = (f32[32,16]{1,0:T(8,128)S(1)}, f32[32,16]{1,0:T(8,128)S(1)}, u32[]{:S(2)}, u32[]{:S(2)}) collective-permute-start(f32[32,16]{1,0:T(8,128)S(1)} %add.47), channel_id=1, source_target_pairs={{0,32},{4,100},{8,40},{12,108},{16,48},{20,116},{24,56},{28,124},{... | collective-permute-start | bytes 6152 | tf_op jit(solution)/shard_map/ppermute | solution.py:515
  46.5 0.1 eq.78
  47.5 0.9 %collective-permute-done.14 = f32[32,16]{1,0:T(8,128)S(1)} collective-permute-done((f32[32,16]{1,0:T(8,128)S(1)}, f32[32,16]{1,0:T(8,128)S(1)}, u32[]{:S(2)}, u32[]{:S(2)}) %collective-permute-start.14) | collective-permute-done | bytes 2080 | tf_op jit(solution)/shard_map/ppermute | solution.py:515
  48.4 1.8 %collective-permute-start.15 = (f32[32,16]{1,0:T(8,128)S(1)}, f32[32,16]{1,0:T(8,128)S(1)}, u32[]{:S(2)}, u32[]{:S(2)}) collective-permute-start(f32[32,16]{1,0:T(8,128)S(1)} %collective-permute-done.14), channel_id=1, source_target_pairs={{0,32},{4,100},{8,40},{12,108},{16,48},{20,116},{24,56},{28,124},{... | collective-permute-start | bytes 6152 | tf_op jit(solution)/shard_map/ppermute | solution.py:516
  50.2 0.7 pad_maximum_fusion
  50.8 2.5 %collective-permute-done.15 = f32[32,16]{1,0:T(8,128)S(1)} collective-permute-done((f32[32,16]{1,0:T(8,128)S(1)}, f32[32,16]{1,0:T(8,128)S(1)}, u32[]{:S(2)}, u32[]{:S(2)}) %collective-permute-start.15) | collective-permute-done | bytes 2080 | tf_op jit(solution)/shard_map/ppermute | solution.py:516
  53.4 2.1 %collective-permute-start.20 = (bf16[256,128]{1,0:T(8,128)(2,1)S(1)}, bf16[256,128]{1,0:T(8,128)(2,1)S(1)}, u32[]{:S(2)}, u32[]{:S(2)}) collective-permute-start(bf16[256,128]{1,0:T(8,128)(2,1)S(1)} %split.9), channel_id=1, source_target_pairs={{0,8},{8,16},{12,4},{16,24},{20,12},{24,32},{28,20},{32,40},{36,28... | collective-permute-start | bytes 196616 | tf_op jit(solution)/shard_map/ppermute | solution.py:575
  55.6 4.6 %place_first.1 = bf16[2,16,512,256]{3,2,1,0:T(8,128)(2,1)} custom-call(s32[512]{0:T(512)S(1)} %copy-done, s32[16]{0:T(128)S(1)} %get-tuple-element.131.refs_1_.refs_0_, bf16[2,16,512,256]{3,2,1,0:T(8,128)(2,1)} %collective-permute-done.17.refs_2_, bf16[2,6,512,256]{3,2,1,0:T(8,128)(2,1)} %collective-permute-done.18.refs_3_, ...), custom_call_target="tpu_custom_call", output_to_operand_aliasing={{}: (4, {})} | custom-call | tf_op jit(solution)/shard_map/place_first/pallas_call | solution.py:176
  60.2 4.0 %collective-permute-start.21 = (f32[32,16]{1,0:T(8,128)S(1)}, f32[32,16]{1,0:T(8,128)S(1)}, u32[]{:S(2)}, u32[]{:S(2)}) collective-permute-start(f32[32,16]{1,0:T(8,128)S(1)} %add_add_fusion.refs_0_), channel_id=1, source_target_pairs={{0,8},{4,12},{8,16},{12,20},{16,24},{20,28},{24,0},{28,4},{32,40},... | collective-permute-start | bytes 6152 | tf_op jit(solution)/shard_map/ppermute | solution.py:524
  64.2 2.9 %collective-permute-start.22 = (f32[32,16]{1,0:T(8,128)S(1)}, f32[32,16]{1,0:T(8,128)S(1)}, u32[]{:S(2)}, u32[]{:S(2)}) collective-permute-start(f32[32,16]{1,0:T(8,128)S(1)} %add_add_fusion.refs_0_), channel_id=1, source_target_pairs={{0,16},{4,20},{8,24},{12,28},{16,0},{20,4},{24,8},{28,12},{32,48},... | collective-permute-start | bytes 6152 | tf_op jit(solution)/shard_map/ppermute | solution.py:524
  67.0 1.6 %collective-permute-start.23 = (f32[32,16]{1,0:T(8,128)S(1)}, f32[32,16]{1,0:T(8,128)S(1)}, u32[]{:S(2)}, u32[]{:S(2)}) collective-permute-start(f32[32,16]{1,0:T(8,128)S(1)} %add_add_fusion.refs_0_), channel_id=1, source_target_pairs={{0,24},{4,28},{8,0},{12,4},{16,8},{20,12},{24,16},{28,20},{32,56},... | collective-permute-start | bytes 6152 | tf_op jit(solution)/shard_map/ppermute | solution.py:524
  68.6 0.1 fusion
  68.8 0.7 reshape.80
  69.4 1.7 %place_more.17 = bf16[2,16,512,256]{3,2,1,0:T(8,128)(2,1)} custom-call(s32[16]{0:T(128)S(1)} %get-tuple-element.131.refs_1_.refs_0_, bf16[2,2,512,256]{3,2,1,0:T(8,128)(2,1)} %collective-permute-done.9.refs_1_, bf16[2,16,512,256]{3,2,1,0:T(8,128)(2,1)} %get-tuple-element.158.refs_2_), custom_call_target="tpu_custom_call", output_to_operand_aliasing={{}: (2, {})} | custom-call | tf_op jit(solution)/shard_map/place_more/pallas_call | solution.py:176
  71.1 0.8 %normalise.1 = f32[1,16]{1,0:T(1,128)} custom-call(f32[32,16]{1,0:T(8,128)S(1)} %add_add_fusion.refs_0_, f32[32,16]{1,0:T(8,128)S(1)} %collective-permute-done.21.refs_1_, f32[32,16]{1,0:T(8,128)S(1)} %collective-permute-done.22.refs_2_, f32[32,16]{1,0:T(8,128)S(1)} %collective-permute-done.23.refs_3_), custom_call_target="tpu_custom_call" | custom-call | tf_op jit(solution)/shard_map/normalise/pallas_call | solution.py:494
  (43 shorter events, 0.8 us)
Async XLA Ops:
  1.7 8.2 %copy-start.1 = (bf16[32,4096]{1,0:T(8,128)(2,1)}, bf16[32,4096]{1,0:T(8,128)(2,1)S(1)}, u32[]{:S(2)}) copy-start(bf16[32,4096]{1,0:T(8,128)(2,1)S(1)} %reshape.78.own) | copy-start | bytes 786436
  1.7 8.2 %collective-permute-start.8 = (bf16[32,4096]{1,0:T(8,128)(2,1)S(1)}, bf16[32,4096]{1,0:T(8,128)(2,1)}, u32[]{:S(2)}, u32[]{:S(2)}) collective-permute-start(bf16[32,4096]{1,0:T(8,128)(2,1)S(1)} %reshape.78.own), channel_id=1, source_target_pairs={{4,8},{8,4},{12,16},{16,12},{20,24},{24,20},{28,32},{32,28},{36,40... | collective-permute-start | bytes 786440 | tf_op jit(solution)/shard_map/ppermute | solution.py:548
  3.1 6.8 %collective-permute-start.10 = (bf16[32,4096]{1,0:T(8,128)(2,1)S(1)}, bf16[32,4096]{1,0:T(8,128)(2,1)}, u32[]{:S(2)}, u32[]{:S(2)}) collective-permute-start(bf16[32,4096]{1,0:T(8,128)(2,1)S(1)} %reshape.78.own), channel_id=1, source_target_pairs={{0,4},{4,0},{8,12},{12,8},{16,20},{20,16},{24,28},{28,24},{32,36},... | collective-permute-start | bytes 786440 | tf_op jit(solution)/shard_map/ppermute | solution.py:549
  7.3 4.9 %copy-start.5 = (f32[16,2]{0,1:T(2,128)S(1)}, f32[16,2]{0,1:T(2,128)}, u32[]{:S(2)}) copy-start(f32[16,2]{0,1:T(2,128)} %param.27) | copy-start | bytes 388
  9.9 45.7 %collective-permute-start.17 = (bf16[2,16,512,256]{3,2,1,0:T(8,128)(2,1)}, bf16[2,16,512,256]{3,2,1,0:T(8,128)(2,1)}, u32[]{:S(2)}, u32[]{:S(2)}) collective-permute-start(bf16[2,16,512,256]{3,2,1,0:T(8,128)(2,1)} %cache.5), channel_id=1, source_target_pairs={{0,4},{4,0},{8,12},{12,8},{16,20},{20,16},{24,28},{28,24},{32,36},... | collective-permute-start | bytes 25165832 | tf_op jit(solution)/shard_map/ppermute | solution.py:560
  10.0 45.6 %collective-permute-start.18 = (bf16[2,6,512,256]{3,2,1,0:T(8,128)(2,1)S(1)}, bf16[2,6,512,256]{3,2,1,0:T(8,128)(2,1)}, u32[]{:S(2)}, u32[]{:S(2)}) collective-permute-start(bf16[2,6,512,256]{3,2,1,0:T(8,128)(2,1)S(1)} %gather.18), channel_id=1, source_target_pairs={{4,8},{8,4},{12,16},{16,12},{20,24},{24,20},{28,32},{32,28},{36,40... | collective-permute-start | bytes 9437192 | tf_op jit(solution)/shard_map/ppermute | solution.py:557
  25.4 2.7 %collective-permute-start.11 = (f32[32,16]{1,0:T(8,128)S(1)}, f32[32,16]{1,0:T(8,128)S(1)}, u32[]{:S(2)}, u32[]{:S(2)}) collective-permute-start(f32[32,16]{1,0:T(8,128)S(1)} %select_select_fusion), channel_id=1, source_target_pairs={{0,4},{4,0},{8,12},{12,8},{16,20},{20,16},{24,28},{28,24},{32,36},... | collective-permute-start | bytes 6152 | tf_op jit(solution)/shard_map/ppermute | solution.py:508
  28.3 6.4 %collective-permute-start.12 = (f32[32,16]{1,0:T(8,128)S(1)}, f32[32,16]{1,0:T(8,128)S(1)}, u32[]{:S(2)}, u32[]{:S(2)}) collective-permute-start(f32[32,16]{1,0:T(8,128)S(1)} %fusion.1), channel_id=1, source_target_pairs={{0,1},{1,0},{2,3},{3,2},{4,5},{5,4},{6,7},{7,6},{8,9},{9,8},{10,11... | collective-permute-start | bytes 6152 | tf_op jit(solution)/shard_map/ppermute | solution.py:511
  30.3 8.2 %copy-start = (s32[512]{0:T(512)S(1)}, s32[512]{0:T(512)}, u32[]{:S(2)}) copy-start(s32[512]{0:T(512)} %refs_0_.1) | copy-start | bytes 6148
  30.3 17.2 %copy-start.4 = (bf16[32,256]{1,0:T(8,128)(2,1)S(1)}, bf16[32,256]{1,0:T(8,128)(2,1)}, u32[]{:S(2)}) copy-start(bf16[32,256]{1,0:T(8,128)(2,1)} %get-tuple-element.147) | copy-start | bytes 49156
  30.3 17.2 %copy-start.3 = (bf16[32,256]{1,0:T(8,128)(2,1)S(1)}, bf16[32,256]{1,0:T(8,128)(2,1)}, u32[]{:S(2)}) copy-start(bf16[32,256]{1,0:T(8,128)(2,1)} %get-tuple-element.146) | copy-start | bytes 49156
  33.0 36.4 %collective-permute-start.9 = (bf16[2,2,512,256]{3,2,1,0:T(8,128)(2,1)}, bf16[2,2,512,256]{3,2,1,0:T(8,128)(2,1)}, u32[]{:S(2)}, u32[]{:S(2)}) collective-permute-start(bf16[2,2,512,256]{3,2,1,0:T(8,128)(2,1)} %gather.19), channel_id=1, source_target_pairs={{4,8},{8,4},{12,16},{16,12},{20,24},{24,20},{28,32},{32,28},{36,40... | collective-permute-start | bytes 3145736 | tf_op jit(solution)/shard_map/ppermute | solution.py:557
  34.8 5.7 %collective-permute-start.13 = (f32[32,16]{1,0:T(8,128)S(1)}, f32[32,16]{1,0:T(8,128)S(1)}, u32[]{:S(2)}, u32[]{:S(2)}) collective-permute-start(f32[32,16]{1,0:T(8,128)S(1)} %fusion.2), channel_id=1, source_target_pairs={{0,2},{1,3},{2,0},{3,1},{4,6},{5,7},{6,4},{7,5},{8,10},{9,11},{10,... | collective-permute-start | bytes 6152 | tf_op jit(solution)/shard_map/ppermute | solution.py:511
  38.6 11.6 %collective-permute-start.19 = (bf16[512,128]{1,0:T(8,128)(2,1)}, bf16[512,128]{1,0:T(8,128)(2,1)S(1)}, u32[]{:S(2)}, u32[]{:S(2)}) collective-permute-start(bf16[512,128]{1,0:T(8,128)(2,1)} %get-tuple-element.149), channel_id=1, source_target_pairs={{0,4},{4,0},{8,12},{12,8},{16,20},{20,16},{24,28},{28,24},{32,36},... | collective-permute-start | bytes 393224 | tf_op jit(solution)/shard_map/ppermute | solution.py:574
  40.5 7.9 %collective-permute-start.14 = (f32[32,16]{1,0:T(8,128)S(1)}, f32[32,16]{1,0:T(8,128)S(1)}, u32[]{:S(2)}, u32[]{:S(2)}) collective-permute-start(f32[32,16]{1,0:T(8,128)S(1)} %add.47), channel_id=1, source_target_pairs={{0,32},{4,100},{8,40},{12,108},{16,48},{20,116},{24,56},{28,124},{... | collective-permute-start | bytes 6152 | tf_op jit(solution)/shard_map/ppermute | solution.py:515
  48.4 4.9 %collective-permute-start.15 = (f32[32,16]{1,0:T(8,128)S(1)}, f32[32,16]{1,0:T(8,128)S(1)}, u32[]{:S(2)}, u32[]{:S(2)}) collective-permute-start(f32[32,16]{1,0:T(8,128)S(1)} %collective-permute-done.14), channel_id=1, source_target_pairs={{0,32},{4,100},{8,40},{12,108},{16,48},{20,116},{24,56},{28,124},{... | collective-permute-start | bytes 6152 | tf_op jit(solution)/shard_map/ppermute | solution.py:516
  50.2 5.3 %collective-permute-start.16 = (f32[32,16]{1,0:T(8,128)S(1)}, f32[32,16]{1,0:T(8,128)S(1)}, u32[]{:S(2)}, u32[]{:S(2)}) collective-permute-start(f32[32,16]{1,0:T(8,128)S(1)} %collective-permute-done.14), channel_id=1, source_target_pairs={{0,4},{4,0},{8,12},{12,8},{16,20},{20,16},{24,28},{28,24},{32,36},... | collective-permute-start | bytes 6152 | tf_op jit(solution)/shard_map/ppermute | solution.py:516
  53.4 15.3 %collective-permute-start.20 = (bf16[256,128]{1,0:T(8,128)(2,1)S(1)}, bf16[256,128]{1,0:T(8,128)(2,1)S(1)}, u32[]{:S(2)}, u32[]{:S(2)}) collective-permute-start(bf16[256,128]{1,0:T(8,128)(2,1)S(1)} %split.9), channel_id=1, source_target_pairs={{0,8},{8,16},{12,4},{16,24},{20,12},{24,32},{28,20},{32,40},{36,28... | collective-permute-start | bytes 196616 | tf_op jit(solution)/shard_map/ppermute | solution.py:575
  55.6 13.1 %copy-start.2 = (bf16[256,128]{1,0:T(8,128)(2,1)S(1)}, bf16[256,128]{1,0:T(8,128)(2,1)}, u32[]{:S(2)}) copy-start(bf16[256,128]{1,0:T(8,128)(2,1)} %get-tuple-element.148) | copy-start | bytes 196612
  60.2 10.9 %collective-permute-start.21 = (f32[32,16]{1,0:T(8,128)S(1)}, f32[32,16]{1,0:T(8,128)S(1)}, u32[]{:S(2)}, u32[]{:S(2)}) collective-permute-start(f32[32,16]{1,0:T(8,128)S(1)} %add_add_fusion.refs_0_), channel_id=1, source_target_pairs={{0,8},{4,12},{8,16},{12,20},{16,24},{20,28},{24,0},{28,4},{32,40},... | collective-permute-start | bytes 6152 | tf_op jit(solution)/shard_map/ppermute | solution.py:524
  64.2 7.0 %collective-permute-start.22 = (f32[32,16]{1,0:T(8,128)S(1)}, f32[32,16]{1,0:T(8,128)S(1)}, u32[]{:S(2)}, u32[]{:S(2)}) collective-permute-start(f32[32,16]{1,0:T(8,128)S(1)} %add_add_fusion.refs_0_), channel_id=1, source_target_pairs={{0,16},{4,20},{8,24},{12,28},{16,0},{20,4},{24,8},{28,12},{32,48},... | collective-permute-start | bytes 6152 | tf_op jit(solution)/shard_map/ppermute | solution.py:524
  67.0 4.1 %collective-permute-start.23 = (f32[32,16]{1,0:T(8,128)S(1)}, f32[32,16]{1,0:T(8,128)S(1)}, u32[]{:S(2)}, u32[]{:S(2)}) collective-permute-start(f32[32,16]{1,0:T(8,128)S(1)} %add_add_fusion.refs_0_), channel_id=1, source_target_pairs={{0,24},{4,28},{8,0},{12,4},{16,8},{20,12},{24,16},{28,20},{32,56},... | collective-permute-start | bytes 6152 | tf_op jit(solution)/shard_map/ppermute | solution.py:524

commit v3 on v2

--- a/solution.py
+++ b/solution.py
@@ -214,10 +214,11 @@
 
 def serve_kernel(
     peers, per_device, heads, groups,
-    ancestors, parent_twist, log_ratio, twist_weight, own, mate, far, cosine, sine, wq, wk, wv, cache,
-    keys, values, out_own, out_others, part, placed,
+    ancestors, picks, parent_twist, log_ratio, twist_weight, own, mate, far, cosine, sine,
+    wq, wk, wv, cache,
+    keys, values, out_own, out_others, spread, placed, sent,
     held, weights_q, weights_k, weights_v, total, turned, tokens, fresh, results,
-    lists, slots, owners, loads, stores, streams,
+    part, lists, slots, owners, loads, stores, streams, sends,
 ):
     d = lax.axis_index("dom")
     first_lane = (lax.axis_index("tp") == 0).astype(jnp.float32)
@@ -284,7 +285,6 @@
             owners[count + extra] = owners[count - 1]
 
     part[...] = jnp.zeros_like(part)
-    part[3 * per_device :, :DECODE_STEPS] = log_ratio[...] * first_lane
     results[...] = jnp.zeros_like(results)
     total[...] = jnp.zeros_like(total)
     per_chunk = per_device // chunks
@@ -417,6 +417,25 @@
 
     loaded = lax.fori_loop(0, (count + AT_ONCE - 1) // AT_ONCE, serve, jnp.int32(0))
     lax.fori_loop(loaded, per_device, arrive, 0)
+    skip = PIECES[0]
+    copies = [
+        pltpu.make_async_copy(held.at[c, picks[skip + i]], sent.at[c, i], sends.at[c, i])
+        for i in range(sent.shape[1])
+        for c in range(2)
+    ]
+    for copy in copies:
+        copy.start()
+    sums = jnp.sum(jnp.transpose(part[...]), 0, keepdims=True)
+    spread[...] = jnp.zeros_like(spread)
+    for h, home in enumerate(homes):
+        share = sums[:, h * per_device : (h + 1) * per_device]
+        if h == 0:
+            share = share + jnp.sum(log_ratio[...], 0, keepdims=True) * first_lane
+
+        @pl.when((home >= 0) & (home < peers))
+        def _():
+            spread[pl.ds(jnp.clip(home, 0, peers - 1), 1), :] = share
+
     out_own[...] = results[:queries, :]
     out_others[...] = results[queries:, :]
 
@@ -431,9 +450,11 @@
         return carry
 
     lax.fori_loop(0, per_device, settle, 0)
-
-
-def serve(ancestors, parent_twist, log_ratio, twist_weight, own, mate, far, wq, wk, wv, cache, peers):
+    for copy in copies:
+        copy.wait()
+
+
+def serve(ancestors, picks, parent_twist, log_ratio, twist_weight, own, mate, far, wq, wk, wv, cache, peers):
     per_device, anchor_point = cache.shape[1:3]
     heads, groups = wq.shape[1] // HEAD_SIZE, wk.shape[1] // HEAD_SIZE
     tile = DECODE_STEPS * heads
@@ -449,11 +470,12 @@
             jax.ShapeDtypeStruct((small, groups * HEAD_SIZE), jnp.bfloat16),
             jax.ShapeDtypeStruct((queries, HEAD_SIZE), jnp.bfloat16),
             jax.ShapeDtypeStruct((2 * queries, HEAD_SIZE), jnp.bfloat16),
-            jax.ShapeDtypeStruct((4 * per_device, HEAD_SIZE), jnp.float32),
+            jax.ShapeDtypeStruct((peers, per_device), jnp.float32),
             pltpu.HBM(cache.shape, cache.dtype),
+            pltpu.HBM((2, PIECES[1], *cache.shape[2:]), cache.dtype),
         ),
-        in_specs=[SMEM, SMEM] + [VMEM] * 7 + [HBM] * 4,
-        out_specs=(VMEM, VMEM, VMEM, VMEM, VMEM, HBM),
+        in_specs=[SMEM, SMEM, SMEM] + [VMEM] * 7 + [HBM] * 4,
+        out_specs=(VMEM, VMEM, VMEM, VMEM, VMEM, HBM, HBM),
         scratch_shapes=[
             pltpu.VMEM(cache.shape, cache.dtype),
             pltpu.VMEM(wq.shape, wq.dtype),
@@ -464,17 +486,22 @@
             pltpu.VMEM((3 * queries, HEAD_SIZE), jnp.bfloat16),
             pltpu.VMEM((3 * 2 * groups * small, HEAD_SIZE), jnp.float32),
             pltpu.VMEM((3 * queries, HEAD_SIZE), jnp.bfloat16),
+            pltpu.VMEM((HEAD_SIZE, HEAD_SIZE), jnp.float32),
             pltpu.SMEM((4 * per_device,), jnp.int32),
             pltpu.SMEM((3 * per_device + AT_ONCE,), jnp.int32),
             pltpu.SMEM((3 * per_device + AT_ONCE,), jnp.int32),
             pltpu.SemaphoreType.DMA((2, per_device)),
             pltpu.SemaphoreType.DMA((2, per_device)),
             pltpu.SemaphoreType.DMA((3, chunks)),
+            pltpu.SemaphoreType.DMA((2, PIECES[1])),
         ],
         compiler_params=pltpu.CompilerParams(vmem_limit_bytes=59 * 2**20),
         cost_estimate=LIGHT,
         name="serve",
-    )(ancestors, parent_twist, log_ratio, twist_weight, own, mate, far, cosine, sine, wq, wk, wv, cache)
+    )(
+        ancestors, picks, parent_twist, log_ratio, twist_weight, own, mate, far, cosine, sine,
+        wq, wk, wv, cache,
+    )
 
 
 def normalise_kernel(terms, *refs):
@@ -548,28 +575,16 @@
     far_rows = lax.ppermute(rows, "dom", off_chip)
     mate_rows = lax.ppermute(rows, "dom", on_chip)
     count, picks, ranks = plan(ancestors, peers, per_device)
-    came, skip = [], 0
-    for size in PIECES:
-        sent = gather(picks, cache, skip, size)
-        if not came:
-            sent, far_rows = lax.optimization_barrier((sent, far_rows))
-        sent, picks = lax.optimization_barrier((sent, picks))
-        came.append(lax.ppermute(sent, "dom", off_chip))
-        skip += size
+    sent, far_rows = lax.optimization_barrier((gather(picks, cache, 0, PIECES[0]), far_rows))
+    first = lax.ppermute(sent, "dom", off_chip)
     late_cache, far_rows, mate_rows = lax.optimization_barrier((cache, far_rows, mate_rows))
     mate_cache = lax.ppermute(late_cache, "dom", on_chip)
-    keys, values, own_part, others_part, part, out = serve(
-        ancestors, parent_twist, log_ratio, twist_weight.reshape(heads, HEAD_SIZE),
+    keys, values, own_part, others_part, spread, out, sent = serve(
+        ancestors, picks, parent_twist, log_ratio.T, twist_weight.reshape(heads, HEAD_SIZE),
         rows, mate_rows, far_rows, query_weight, key_projection_weight, value_projection_weight,
         cache, peers,
     )
-    part = jnp.sum(part, 1).reshape(4, per_device)
-    index = jnp.arange(peers)[:, None]
-    spread = jnp.where(
-        index == d,
-        part[0] + part[3],
-        jnp.where(index == chip_mate(d), part[1], jnp.where(index == next_chip(d), part[2], 0.0)),
-    )
+    second = lax.ppermute(sent, "dom", off_chip)
     spread = total_but_y(spread, peers)
     mate_part, far_part = jnp.split(lax.ppermute(others_part, "dom", on_chip), 2)
     far_part = lax.ppermute(far_part, "dom", beside)
@@ -578,7 +593,7 @@
     attention = jnp.where(
         owner == d, own_part, jnp.where(owner == chip_mate(d), mate_part, far_part)
     ).reshape(per_device, DECODE_STEPS, heads * HEAD_SIZE)
-    out = place_first(ancestors, ranks, mate_cache, came[0], out)
+    out = place_first(ancestors, ranks, mate_cache, first, out)
     spread, out = lax.optimization_barrier((spread, out))
     log_weights = normalise(parts_along_y(spread, peers)).reshape(per_device)
     fresh = jnp.stack([keys, values]).reshape(2, per_device, DECODE_STEPS, groups * HEAD_SIZE)
@@ -595,10 +610,7 @@
         [lambda cache, picks, ranks, out: out] + [more(i + 1) for i in range(per_device - ALWAYS)],
         cache, picks, ranks, out,
     )
-    skip = PIECES[0]
-    for piece in came[1:]:
-        out = place_more(ranks, piece, out, skip)
-        skip += piece.shape[1]
+    out = place_more(ranks, second, out, PIECES[0])
     return (out, fresh, attention, log_weights)
 
 

time: 72.1 us -> 70.4 us (0.976); the launches traced: 71.9 us -> 69.3 us
  starting transfers between devices: 35.6 us -> 31.3 us
  waiting for transfers between devices: 4.32 us -> 7.58 us
  Pallas kernels: 25.6 us -> 23.8 us
  local copies, waits for them, and re-layouts: 2.77 us -> 3.51 us
    ppermute x2, waiting for transfers between devices: 0.01 us -> 3.39 us  [total_but_y(): x = x + lax.ppermute(x, 'tp', [(i, i ^ hop) for i in range(ring)])]
    pallas_call x2 -> x1, Pallas kernels: 5.24 us -> 2.48 us  [gather(): pl.pallas_call(functools.partial(gather_kernel, skip, size), out_shape=pl...]
    ppermute x1, starting transfers between devices: 1.97 us -> 0.05 us  [shards(): lax.ppermute(others_part, 'dom', on_chip)]
    another operation x2, local copies, waits for them, and re-layouts: 0.03 us -> 1.46 us  [shards(): jnp.stack([keys, values])]
    ppermute x3, waiting for transfers between devices: 0.01 us -> 1.24 us  [parts_along_y(): parts.append(lax.ppermute(x, 'dom', pairs))]
    pallas_call x1, Pallas kernels: 11.4 us -> 12.6 us  [serve(): pl.pallas_call(functools.partial(serve_kernel, peers, per_device, heads,...]
    ppermute x3, starting transfers between devices: 8.42 us -> 7.47 us  [parts_along_y(): parts.append(lax.ppermute(x, 'dom', pairs))]
    ppermute x1, waiting for transfers between devices: 0.93 us -> 0.01 us  [total_but_y(): first = lax.ppermute(x, 'dom', pairs)]
  transfers between devices with their start and end apart: 16 -> 16, of which waited for: 3 -> 5; matrix products, arithmetic and copies ran while one was open for 5% -> 6% of each run, Pallas kernels for 35% -> 33%
where the time goes in v3:
time: 70.4 us; the launch traced here: 69.3 us
  starting transfers between devices  31.3 us (44%)
  Pallas kernels  23.8 us (34%)
  waiting for transfers between devices  7.58 us (11%)
  local copies, waits for them, and re-layouts  3.51 us (5%)
  other arithmetic  1.63 us (2%)
  between operations  1.48 us (2%)
    pallas_call x1, Pallas kernels, serve(): pl.pallas_call(functools.partial(serve_kernel, peers, per_device, heads,...  12.6 us
    ppermute x3, starting transfers between devices, parts_along_y(): parts.append(lax.ppermute(x, 'dom', pairs))  7.47 us
    pallas_call x2, Pallas kernels, place(): pl.pallas_call(functools.partial(place_kernel, per_device, find, len(numb...  6.12 us
    ppermute x2, starting transfers between devices, total_but_y(): x = x + lax.ppermute(x, 'tp', [(i, i ^ hop) for i in range(ring)])  5.8 us
    ppermute x1, starting transfers between devices, total_but_y(): first = lax.ppermute(x, 'dom', pairs)  5.67 us
    ppermute x2, waiting for transfers between devices, total_but_y(): x = x + lax.ppermute(x, 'tp', [(i, i ^ hop) for i in range(ring)])  3.39 us
    pallas_call x1, Pallas kernels, gather(): pl.pallas_call(functools.partial(gather_kernel, skip, size), out_shape=pl...  2.48 us
    ppermute x1, starting transfers between devices, shards(): mate_rows = lax.ppermute(rows, 'dom', on_chip)  2.41 us
  transfers between devices with their start and end apart: 16, of which 5 were waited for; matrix products, arithmetic and copies ran while one was open for 6% of the time, Pallas kernels for 33%

profile of v3, /device:TPU:0, one launch (start us, length us, event | category | flops | bytes accessed | tf_op | source)
XLA Modules:
  0.0 69.3 jit_solution(4494432299325807137)
XLA Ops:
  0.6 1.0 %reshape.55.own = bf16[32,4096]{1,0:T(8,128)(2,1)S(1)} reshape(bf16[16,2,4096]{2,1,0:T(2,128)(2,1)} %param.21) | data formatting | bytes 524288 | tf_op jit(solution)/shard_map/reshape | solution.py:574
  1.7 1.4 %collective-permute-start.8 = (bf16[32,4096]{1,0:T(8,128)(2,1)S(1)}, bf16[32,4096]{1,0:T(8,128)(2,1)}, u32[]{:S(2)}, u32[]{:S(2)}) collective-permute-start(bf16[32,4096]{1,0:T(8,128)(2,1)S(1)} %reshape.55.own), channel_id=1, source_target_pairs={{4,8},{8,4},{12,16},{16,12},{20,24},{24,20},{28,32},{32,28},{36,40... | collective-permute-start | bytes 786440 | tf_op jit(solution)/shard_map/ppermute | solution.py:575
  3.1 2.4 %collective-permute-start.9 = (bf16[32,4096]{1,0:T(8,128)(2,1)S(1)}, bf16[32,4096]{1,0:T(8,128)(2,1)}, u32[]{:S(2)}, u32[]{:S(2)}) collective-permute-start(bf16[32,4096]{1,0:T(8,128)(2,1)S(1)} %reshape.55.own), channel_id=1, source_target_pairs={{0,4},{4,0},{8,12},{12,8},{16,20},{20,16},{24,28},{28,24},{32,36},... | collective-permute-start | bytes 786440 | tf_op jit(solution)/shard_map/ppermute | solution.py:576
  5.5 1.9 %plan.1 = (s32[1]{0:T(128)}, s32[16]{0:T(128)S(1)}, s32[16]{0:T(128)S(1)}) custom-call(s32[512]{0:T(512)} %refs_0_.1, s32[4,128]{1,0:T(4,128)} %bitcast.5), custom_call_target="tpu_custom_call" | custom-call | tf_op jit(solution)/shard_map/plan/pallas_call | solution.py:96
  7.3 2.5 %gather.17 = bf16[2,6,512,256]{3,2,1,0:T(8,128)(2,1)S(1)} custom-call(s32[16]{0:T(128)S(1)} %get-tuple-element.129.picks, bf16[2,16,512,256]{3,2,1,0:T(8,128)(2,1)} %cache.3), custom_call_target="tpu_custom_call" | custom-call | tf_op jit(solution)/shard_map/gather/pallas_call | solution.py:128
  9.9 0.1 collective-permute-start.17
  10.0 2.3 %collective-permute-start.18 = (bf16[2,6,512,256]{3,2,1,0:T(8,128)(2,1)S(1)}, bf16[2,6,512,256]{3,2,1,0:T(8,128)(2,1)}, u32[]{:S(2)}, u32[]{:S(2)}) collective-permute-start(bf16[2,6,512,256]{3,2,1,0:T(8,128)(2,1)S(1)} %gather.17), channel_id=1, source_target_pairs={{4,8},{8,4},{12,16},{16,12},{20,24},{24,20},{28,32},{32,28},{36,40... | collective-permute-start | bytes 9437192 | tf_op jit(solution)/shard_map/ppermute | solution.py:579
  12.3 12.6 %serve.1 = (bf16[32,256]{1,0:T(8,128)(2,1)}, bf16[32,256]{1,0:T(8,128)(2,1)}, bf16[256,128]{1,0:T(8,128)(2,1)}, bf16[512,128]{1,0:T(8,128)(2,1)}, f32[32,16]{1,0...) custom-call(s32[512]{0:T(512)} %refs_0_.1, s32[16]{0:T(128)S(1)} %get-tuple-element.129.picks, ...), custom_call_target="tpu_custom_call" | custom-call | tf_op jit(solution)/shard_map/serve/pallas_call | solution.py:466
  24.9 1.7 %collective-permute-start.10 = (bf16[2,2,512,256]{3,2,1,0:T(8,128)(2,1)}, bf16[2,2,512,256]{3,2,1,0:T(8,128)(2,1)}, u32[]{:S(2)}, u32[]{:S(2)}) collective-permute-start(bf16[2,2,512,256]{3,2,1,0:T(8,128)(2,1)} %get-tuple-element.133), channel_id=1, source_target_pairs={{4,8},{8,4},{12,16},{16,12},{20,24},{24,20},{28,32},{32,28},{36,40... | collective-permute-start | bytes 3145736 | tf_op jit(solution)/shard_map/ppermute | solution.py:587
  26.5 1.9 %collective-permute-start.11 = (f32[32,16]{1,0:T(8,128)}, f32[32,16]{1,0:T(8,128)S(1)}, u32[]{:S(2)}, u32[]{:S(2)}) collective-permute-start(f32[32,16]{1,0:T(8,128)} %get-tuple-element.135), channel_id=1, source_target_pairs={{0,4},{4,0},{8,12},{12,8},{16,20},{20,16},{24,28},{28,24},{32,36},... | collective-permute-start | bytes 6152 | tf_op jit(solution)/shard_map/ppermute | solution.py:535
  28.4 1.0 %collective-permute-done.11 = f32[32,16]{1,0:T(8,128)S(1)} collective-permute-done((f32[32,16]{1,0:T(8,128)}, f32[32,16]{1,0:T(8,128)S(1)}, u32[]{:S(2)}, u32[]{:S(2)}) %collective-permute-start.11) | collective-permute-done | bytes 2080 | tf_op jit(solution)/shard_map/ppermute | solution.py:535
  29.5 0.7 %add.31 = f32[32,16]{1,0:T(8,128)S(1)} add(f32[32,16]{1,0:T(8,128)} %get-tuple-element.135, f32[32,16]{1,0:T(8,128)S(1)} %collective-permute-done.11) | non-fusion elementwise | flops 512 | bytes 6144 | tf_op jit(solution)/shard_map/add | solution.py:535
  30.2 1.9 %collective-permute-start.12 = (f32[32,16]{1,0:T(8,128)S(1)}, f32[32,16]{1,0:T(8,128)S(1)}, u32[]{:S(2)}, u32[]{:S(2)}) collective-permute-start(f32[32,16]{1,0:T(8,128)S(1)} %add.31), channel_id=1, source_target_pairs={{0,1},{1,0},{2,3},{3,2},{4,5},{5,4},{6,7},{7,6},{8,9},{9,8},{10,11... | collective-permute-start | bytes 6152 | tf_op jit(solution)/shard_map/ppermute | solution.py:538
  32.1 1.8 %collective-permute-done.12 = f32[32,16]{1,0:T(8,128)S(1)} collective-permute-done((f32[32,16]{1,0:T(8,128)S(1)}, f32[32,16]{1,0:T(8,128)S(1)}, u32[]{:S(2)}, u32[]{:S(2)}) %collective-permute-start.12) | collective-permute-done | bytes 2080 | tf_op jit(solution)/shard_map/ppermute | solution.py:538
  34.0 3.9 %collective-permute-start.13 = (f32[32,16]{1,0:T(8,128)S(1)}, f32[32,16]{1,0:T(8,128)S(1)}, u32[]{:S(2)}, u32[]{:S(2)}) collective-permute-start(f32[32,16]{1,0:T(8,128)S(1)} %add.32), channel_id=1, source_target_pairs={{0,2},{1,3},{2,0},{3,1},{4,6},{5,7},{6,4},{7,5},{8,10},{9,11},{10,... | collective-permute-start | bytes 6152 | tf_op jit(solution)/shard_map/ppermute | solution.py:538
  38.0 1.6 %collective-permute-done.13 = f32[32,16]{1,0:T(8,128)S(1)} collective-permute-done((f32[32,16]{1,0:T(8,128)S(1)}, f32[32,16]{1,0:T(8,128)S(1)}, u32[]{:S(2)}, u32[]{:S(2)}) %collective-permute-start.13) | collective-permute-done | bytes 2080 | tf_op jit(solution)/shard_map/ppermute | solution.py:538
  39.6 5.7 %collective-permute-start.14 = (f32[32,16]{1,0:T(8,128)S(1)}, f32[32,16]{1,0:T(8,128)S(1)}, u32[]{:S(2)}, u32[]{:S(2)}) collective-permute-start(f32[32,16]{1,0:T(8,128)S(1)} %add.33), channel_id=1, source_target_pairs={{0,32},{4,100},{8,40},{12,108},{16,48},{20,116},{24,56},{28,124},{... | collective-permute-start | bytes 6152 | tf_op jit(solution)/shard_map/ppermute | solution.py:542
  45.3 0.1 eq.37
  46.2 0.7 %stack.10 = bf16[1,16,2,256]{3,2,1,0:T(2,128)(2,1)S(1)} reshape(bf16[32,256]{1,0:T(8,128)(2,1)} %get-tuple-element.141) | data formatting | bytes 32768 | tf_op jit(solution)/shard_map/stack | solution.py:599
  47.0 0.7 %stack.9 = bf16[1,16,2,256]{3,2,1,0:T(2,128)(2,1)S(1)} reshape(bf16[32,256]{1,0:T(8,128)(2,1)} %get-tuple-element.140) | data formatting | bytes 32768 | tf_op jit(solution)/shard_map/stack | solution.py:599
  47.8 1.2 %collective-permute-start.15 = (f32[32,16]{1,0:T(8,128)S(1)}, f32[32,16]{1,0:T(8,128)S(1)}, u32[]{:S(2)}, u32[]{:S(2)}) collective-permute-start(f32[32,16]{1,0:T(8,128)S(1)} %collective-permute-done.14), channel_id=1, source_target_pairs={{0,32},{4,100},{8,40},{12,108},{16,48},{20,116},{24,56},{28,124},{... | collective-permute-start | bytes 6152 | tf_op jit(solution)/shard_map/ppermute | solution.py:543
  49.0 0.7 pad_maximum_fusion
  49.6 1.3 %collective-permute-start.20 = (bf16[256,128]{1,0:T(8,128)(2,1)S(1)}, bf16[256,128]{1,0:T(8,128)(2,1)S(1)}, u32[]{:S(2)}, u32[]{:S(2)}) collective-permute-start(bf16[256,128]{1,0:T(8,128)(2,1)S(1)} %split.9), channel_id=1, source_target_pairs={{0,8},{8,16},{12,4},{16,24},{20,12},{24,32},{28,20},{32,40},{36,28... | collective-permute-start | bytes 196616 | tf_op jit(solution)/shard_map/ppermute | solution.py:590
  51.0 1.9 %collective-permute-done.15 = f32[32,16]{1,0:T(8,128)S(1)} collective-permute-done((f32[32,16]{1,0:T(8,128)S(1)}, f32[32,16]{1,0:T(8,128)S(1)}, u32[]{:S(2)}, u32[]{:S(2)}) %collective-permute-start.15) | collective-permute-done | bytes 2080 | tf_op jit(solution)/shard_map/ppermute | solution.py:543
  52.9 4.5 %place_first.1 = bf16[2,16,512,256]{3,2,1,0:T(8,128)(2,1)} custom-call(s32[512]{0:T(512)S(1)} %copy-done, s32[16]{0:T(128)S(1)} %get-tuple-element.128.refs_1_.refs_0_, bf16[2,16,512,256]{3,2,1,0:T(8,128)(2,1)} %collective-permute-done.17.refs_2_, bf16[2,6,512,256]{3,2,1,0:T(8,128)(2,1)} %collective-permute-done.18.refs_3_, ...), custom_call_target="tpu_custom_call", output_to_operand_aliasing={{}: (4, {})} | custom-call | tf_op jit(solution)/shard_map/place_first/pallas_call | solution.py:176
  57.3 1.9 %collective-permute-start.21 = (f32[32,16]{1,0:T(8,128)S(1)}, f32[32,16]{1,0:T(8,128)S(1)}, u32[]{:S(2)}, u32[]{:S(2)}) collective-permute-start(f32[32,16]{1,0:T(8,128)S(1)} %add_add_fusion.refs_0_), channel_id=1, source_target_pairs={{0,8},{4,12},{8,16},{12,20},{16,24},{20,28},{24,0},{28,4},{32,40},... | collective-permute-start | bytes 6152 | tf_op jit(solution)/shard_map/ppermute | solution.py:551
  59.2 5.6 %collective-permute-start.22 = (f32[32,16]{1,0:T(8,128)S(1)}, f32[32,16]{1,0:T(8,128)S(1)}, u32[]{:S(2)}, u32[]{:S(2)}) collective-permute-start(f32[32,16]{1,0:T(8,128)S(1)} %add_add_fusion.refs_0_), channel_id=1, source_target_pairs={{0,16},{4,20},{8,24},{12,28},{16,0},{20,4},{24,8},{28,12},{32,48},... | collective-permute-start | bytes 6152 | tf_op jit(solution)/shard_map/ppermute | solution.py:551
  64.8 0.1 fusion
  65.0 0.7 reshape.56
  65.6 1.7 %place_more.17 = bf16[2,16,512,256]{3,2,1,0:T(8,128)(2,1)} custom-call(s32[16]{0:T(128)S(1)} %get-tuple-element.128.refs_1_.refs_0_, bf16[2,2,512,256]{3,2,1,0:T(8,128)(2,1)} %collective-permute-done.10.refs_1_, bf16[2,16,512,256]{3,2,1,0:T(8,128)(2,1)} %get-tuple-element.147.refs_2_), custom_call_target="tpu_custom_call", output_to_operand_aliasing={{}: (2, {})} | custom-call | tf_op jit(solution)/shard_map/place_more/pallas_call | solution.py:176
  67.3 1.2 %collective-permute-done.23.refs_3_ = f32[32,16]{1,0:T(8,128)S(1)} collective-permute-done((f32[32,16]{1,0:T(8,128)S(1)}, f32[32,16]{1,0:T(8,128)S(1)}, u32[]{:S(2)}, u32[]{:S(2)}) %collective-permute-start.23) | collective-permute-done | bytes 2080 | tf_op jit(solution)/shard_map/ppermute | solution.py:551
  68.5 0.8 %normalise.1 = f32[1,16]{1,0:T(1,128)} custom-call(f32[32,16]{1,0:T(8,128)S(1)} %add_add_fusion.refs_0_, f32[32,16]{1,0:T(8,128)S(1)} %collective-permute-done.21.refs_1_, f32[32,16]{1,0:T(8,128)S(1)} %collective-permute-done.22.refs_2_, f32[32,16]{1,0:T(8,128)S(1)} %collective-permute-done.23.refs_3_), custom_call_target="tpu_custom_call" | custom-call | tf_op jit(solution)/shard_map/normalise/pallas_call | solution.py:521
  (30 shorter events, 0.5 us)
Async XLA Ops:
  1.7 8.1 %copy-start.1 = (bf16[32,4096]{1,0:T(8,128)(2,1)}, bf16[32,4096]{1,0:T(8,128)(2,1)S(1)}, u32[]{:S(2)}) copy-start(bf16[32,4096]{1,0:T(8,128)(2,1)S(1)} %reshape.55.own) | copy-start | bytes 786436
  1.7 8.1 %collective-permute-start.8 = (bf16[32,4096]{1,0:T(8,128)(2,1)S(1)}, bf16[32,4096]{1,0:T(8,128)(2,1)}, u32[]{:S(2)}, u32[]{:S(2)}) collective-permute-start(bf16[32,4096]{1,0:T(8,128)(2,1)S(1)} %reshape.55.own), channel_id=1, source_target_pairs={{4,8},{8,4},{12,16},{16,12},{20,24},{24,20},{28,32},{32,28},{36,40... | collective-permute-start | bytes 786440 | tf_op jit(solution)/shard_map/ppermute | solution.py:575
  3.1 6.8 %collective-permute-start.9 = (bf16[32,4096]{1,0:T(8,128)(2,1)S(1)}, bf16[32,4096]{1,0:T(8,128)(2,1)}, u32[]{:S(2)}, u32[]{:S(2)}) collective-permute-start(bf16[32,4096]{1,0:T(8,128)(2,1)S(1)} %reshape.55.own), channel_id=1, source_target_pairs={{0,4},{4,0},{8,12},{12,8},{16,20},{20,16},{24,28},{28,24},{32,36},... | collective-permute-start | bytes 786440 | tf_op jit(solution)/shard_map/ppermute | solution.py:576
  9.9 43.0 %collective-permute-start.17 = (bf16[2,16,512,256]{3,2,1,0:T(8,128)(2,1)}, bf16[2,16,512,256]{3,2,1,0:T(8,128)(2,1)}, u32[]{:S(2)}, u32[]{:S(2)}) collective-permute-start(bf16[2,16,512,256]{3,2,1,0:T(8,128)(2,1)} %cache.3), channel_id=1, source_target_pairs={{0,4},{4,0},{8,12},{12,8},{16,20},{20,16},{24,28},{28,24},{32,36},... | collective-permute-start | bytes 25165832 | tf_op jit(solution)/shard_map/ppermute | solution.py:581
  10.0 42.9 %collective-permute-start.18 = (bf16[2,6,512,256]{3,2,1,0:T(8,128)(2,1)S(1)}, bf16[2,6,512,256]{3,2,1,0:T(8,128)(2,1)}, u32[]{:S(2)}, u32[]{:S(2)}) collective-permute-start(bf16[2,6,512,256]{3,2,1,0:T(8,128)(2,1)S(1)} %gather.17), channel_id=1, source_target_pairs={{4,8},{8,4},{12,16},{16,12},{20,24},{24,20},{28,32},{32,28},{36,40... | collective-permute-start | bytes 9437192 | tf_op jit(solution)/shard_map/ppermute | solution.py:579
  12.3 25.5 %copy-start = (s32[512]{0:T(512)S(1)}, s32[512]{0:T(512)}, u32[]{:S(2)}) copy-start(s32[512]{0:T(512)} %refs_0_.1) | copy-start | bytes 6148
  24.9 40.7 %collective-permute-start.10 = (bf16[2,2,512,256]{3,2,1,0:T(8,128)(2,1)}, bf16[2,2,512,256]{3,2,1,0:T(8,128)(2,1)}, u32[]{:S(2)}, u32[]{:S(2)}) collective-permute-start(bf16[2,2,512,256]{3,2,1,0:T(8,128)(2,1)} %get-tuple-element.133), channel_id=1, source_target_pairs={{4,8},{8,4},{12,16},{16,12},{20,24},{24,20},{28,32},{32,28},{36,40... | collective-permute-start | bytes 3145736 | tf_op jit(solution)/shard_map/ppermute | solution.py:587
  26.5 3.0 %collective-permute-start.11 = (f32[32,16]{1,0:T(8,128)}, f32[32,16]{1,0:T(8,128)S(1)}, u32[]{:S(2)}, u32[]{:S(2)}) collective-permute-start(f32[32,16]{1,0:T(8,128)} %get-tuple-element.135), channel_id=1, source_target_pairs={{0,4},{4,0},{8,12},{12,8},{16,20},{20,16},{24,28},{28,24},{32,36},... | collective-permute-start | bytes 6152 | tf_op jit(solution)/shard_map/ppermute | solution.py:535
  30.2 3.7 %collective-permute-start.12 = (f32[32,16]{1,0:T(8,128)S(1)}, f32[32,16]{1,0:T(8,128)S(1)}, u32[]{:S(2)}, u32[]{:S(2)}) collective-permute-start(f32[32,16]{1,0:T(8,128)S(1)} %add.31), channel_id=1, source_target_pairs={{0,1},{1,0},{2,3},{3,2},{4,5},{5,4},{6,7},{7,6},{8,9},{9,8},{10,11... | collective-permute-start | bytes 6152 | tf_op jit(solution)/shard_map/ppermute | solution.py:538
  34.0 5.6 %collective-permute-start.13 = (f32[32,16]{1,0:T(8,128)S(1)}, f32[32,16]{1,0:T(8,128)S(1)}, u32[]{:S(2)}, u32[]{:S(2)}) collective-permute-start(f32[32,16]{1,0:T(8,128)S(1)} %add.32), channel_id=1, source_target_pairs={{0,2},{1,3},{2,0},{3,1},{4,6},{5,7},{6,4},{7,5},{8,10},{9,11},{10,... | collective-permute-start | bytes 6152 | tf_op jit(solution)/shard_map/ppermute | solution.py:538
  37.9 9.9 %collective-permute-start.19 = (bf16[512,128]{1,0:T(8,128)(2,1)}, bf16[512,128]{1,0:T(8,128)(2,1)S(1)}, u32[]{:S(2)}, u32[]{:S(2)}) collective-permute-start(bf16[512,128]{1,0:T(8,128)(2,1)} %get-tuple-element.143), channel_id=1, source_target_pairs={{0,4},{4,0},{8,12},{12,8},{16,20},{20,16},{24,28},{28,24},{32,36},... | collective-permute-start | bytes 393224 | tf_op jit(solution)/shard_map/ppermute | solution.py:589
  39.6 8.1 %collective-permute-start.14 = (f32[32,16]{1,0:T(8,128)S(1)}, f32[32,16]{1,0:T(8,128)S(1)}, u32[]{:S(2)}, u32[]{:S(2)}) collective-permute-start(f32[32,16]{1,0:T(8,128)S(1)} %add.33), channel_id=1, source_target_pairs={{0,32},{4,100},{8,40},{12,108},{16,48},{20,116},{24,56},{28,124},{... | collective-permute-start | bytes 6152 | tf_op jit(solution)/shard_map/ppermute | solution.py:542
  47.7 1.9 %collective-permute-start.16 = (f32[32,16]{1,0:T(8,128)S(1)}, f32[32,16]{1,0:T(8,128)S(1)}, u32[]{:S(2)}, u32[]{:S(2)}) collective-permute-start(f32[32,16]{1,0:T(8,128)S(1)} %collective-permute-done.14), channel_id=1, source_target_pairs={{0,4},{4,0},{8,12},{12,8},{16,20},{20,16},{24,28},{28,24},{32,36},... | collective-permute-start | bytes 6152 | tf_op jit(solution)/shard_map/ppermute | solution.py:543
  47.8 5.0 %collective-permute-start.15 = (f32[32,16]{1,0:T(8,128)S(1)}, f32[32,16]{1,0:T(8,128)S(1)}, u32[]{:S(2)}, u32[]{:S(2)}) collective-permute-start(f32[32,16]{1,0:T(8,128)S(1)} %collective-permute-done.14), channel_id=1, source_target_pairs={{0,32},{4,100},{8,40},{12,108},{16,48},{20,116},{24,56},{28,124},{... | collective-permute-start | bytes 6152 | tf_op jit(solution)/shard_map/ppermute | solution.py:543
  49.6 15.2 %collective-permute-start.20 = (bf16[256,128]{1,0:T(8,128)(2,1)S(1)}, bf16[256,128]{1,0:T(8,128)(2,1)S(1)}, u32[]{:S(2)}, u32[]{:S(2)}) collective-permute-start(bf16[256,128]{1,0:T(8,128)(2,1)S(1)} %split.9), channel_id=1, source_target_pairs={{0,8},{8,16},{12,4},{16,24},{20,12},{24,32},{28,20},{32,40},{36,28... | collective-permute-start | bytes 196616 | tf_op jit(solution)/shard_map/ppermute | solution.py:590
  52.9 12.0 %copy-start.2 = (bf16[256,128]{1,0:T(8,128)(2,1)S(1)}, bf16[256,128]{1,0:T(8,128)(2,1)}, u32[]{:S(2)}) copy-start(bf16[256,128]{1,0:T(8,128)(2,1)} %get-tuple-element.142) | copy-start | bytes 196612
  57.3 10.0 %collective-permute-start.21 = (f32[32,16]{1,0:T(8,128)S(1)}, f32[32,16]{1,0:T(8,128)S(1)}, u32[]{:S(2)}, u32[]{:S(2)}) collective-permute-start(f32[32,16]{1,0:T(8,128)S(1)} %add_add_fusion.refs_0_), channel_id=1, source_target_pairs={{0,8},{4,12},{8,16},{12,20},{16,24},{20,28},{24,0},{28,4},{32,40},... | collective-permute-start | bytes 6152 | tf_op jit(solution)/shard_map/ppermute | solution.py:551
  59.2 8.1 %collective-permute-start.22 = (f32[32,16]{1,0:T(8,128)S(1)}, f32[32,16]{1,0:T(8,128)S(1)}, u32[]{:S(2)}, u32[]{:S(2)}) collective-permute-start(f32[32,16]{1,0:T(8,128)S(1)} %add_add_fusion.refs_0_), channel_id=1, source_target_pairs={{0,16},{4,20},{8,24},{12,28},{16,0},{20,4},{24,8},{28,12},{32,48},... | collective-permute-start | bytes 6152 | tf_op jit(solution)/shard_map/ppermute | solution.py:551
  64.8 3.7 %collective-permute-start.23 = (f32[32,16]{1,0:T(8,128)S(1)}, f32[32,16]{1,0:T(8,128)S(1)}, u32[]{:S(2)}, u32[]{:S(2)}) collective-permute-start(f32[32,16]{1,0:T(8,128)S(1)} %add_add_fusion.refs_0_), channel_id=1, source_target_pairs={{0,24},{4,28},{8,0},{12,4},{16,8},{20,12},{24,16},{28,20},{32,56},... | collective-permute-start | bytes 6152 | tf_op jit(solution)/shard_map/ppermute | solution.py:551

commit v4 on v3

--- a/solution.py
+++ b/solution.py
@@ -102,6 +102,7 @@
         ),
         in_specs=[SMEM, VMEM],
         out_specs=(SMEM, SMEM, SMEM),
+        compiler_params=SMALL,
         cost_estimate=LIGHT,
         name="plan",
     )(ancestors, ancestors.reshape(-1, 128))
@@ -217,8 +218,8 @@
     ancestors, picks, parent_twist, log_ratio, twist_weight, own, mate, far, cosine, sine,
     wq, wk, wv, cache,
     keys, values, out_own, out_others, spread, placed, sent,
-    held, weights_q, weights_k, weights_v, total, turned, tokens, fresh, results,
-    part, lists, slots, owners, loads, stores, streams, sends,
+    held, total, turned, tokens, fresh, results,
+    part, lists, slots, owners, loads, stores, sends,
 ):
     d = lax.axis_index("dom")
     first_lane = (lax.axis_index("tp") == 0).astype(jnp.float32)
@@ -227,20 +228,8 @@
     small = per_device * DECODE_STEPS
     homes = (d, chip_mate(d), next_chip(d))
     width_q, width_k = heads * HEAD_SIZE, groups * HEAD_SIZE
-    chunks = streams.shape[1]
+    chunks = 8
     depth = wq.shape[0] // chunks
-
-    def stream(i, k):
-        rows = pl.ds(pl.multiple_of(k * depth, depth), depth)
-        source, target = ((wq, weights_q), (wk, weights_k), (wv, weights_v))[i]
-        return pltpu.make_async_copy(source.at[rows, :], target.at[rows, :], streams.at[i, k])
-
-    def begin(k, carry):
-        for i in range(3):
-            stream(i, k).start()
-        return carry
-
-    lax.fori_loop(0, chunks, begin, 0)
 
     def load(j, c):
         return pltpu.make_async_copy(cache.at[c, j], held.at[c, j], loads.at[c, j])
@@ -290,15 +279,13 @@
     per_chunk = per_device // chunks
 
     def project(k, carry):
-        for i in range(3):
-            stream(i, k).wait()
         for j in range(per_chunk):
             for c in range(2):
                 load(k * per_chunk + j, c).start()
         at = pl.ds(pl.multiple_of(k * depth, depth), depth)
         rows = jnp.concatenate([own[:, at], mate[:, at], far[:, at]], 0)
         lanes = 0
-        for weight, width in ((weights_q, width_q), (weights_k, width_k), (weights_v, width_k)):
+        for weight, width in ((wq, width_q), (wk, width_k), (wv, width_k)):
             total[:, lanes : lanes + width] += jnp.dot(
                 rows, weight[at, :], preferred_element_type=jnp.float32
             )
@@ -462,7 +449,6 @@
     small = per_device * DECODE_STEPS
     cosine, sine = rope_tables(small, anchor_point)
     columns = wq.shape[1] + wk.shape[1] + wv.shape[1]
-    chunks = 8
     return pl.pallas_call(
         functools.partial(serve_kernel, peers, per_device, heads, groups),
         out_shape=(
@@ -474,13 +460,10 @@
             pltpu.HBM(cache.shape, cache.dtype),
             pltpu.HBM((2, PIECES[1], *cache.shape[2:]), cache.dtype),
         ),
-        in_specs=[SMEM, SMEM, SMEM] + [VMEM] * 7 + [HBM] * 4,
+        in_specs=[SMEM, SMEM, SMEM] + [VMEM] * 10 + [HBM],
         out_specs=(VMEM, VMEM, VMEM, VMEM, VMEM, HBM, HBM),
         scratch_shapes=[
             pltpu.VMEM(cache.shape, cache.dtype),
-            pltpu.VMEM(wq.shape, wq.dtype),
-            pltpu.VMEM(wk.shape, wk.dtype),
-            pltpu.VMEM(wv.shape, wv.dtype),
             pltpu.VMEM((3 * small, columns), jnp.float32),
             pltpu.VMEM((small, heads, HEAD_SIZE), jnp.float32),
             pltpu.VMEM((3 * queries, HEAD_SIZE), jnp.bfloat16),
@@ -492,10 +475,9 @@
             pltpu.SMEM((3 * per_device + AT_ONCE,), jnp.int32),
             pltpu.SemaphoreType.DMA((2, per_device)),
             pltpu.SemaphoreType.DMA((2, per_device)),
-            pltpu.SemaphoreType.DMA((3, chunks)),
             pltpu.SemaphoreType.DMA((2, PIECES[1])),
         ],
-        compiler_params=pltpu.CompilerParams(vmem_limit_bytes=59 * 2**20),
+        compiler_params=pltpu.CompilerParams(vmem_limit_bytes=28 * 2**20),
         cost_estimate=LIGHT,
         name="serve",
     )(

time: 70.4 us -> 68.8 us (0.977)
  the two profiles are of different devices: /device:TPU:0 before, /device:TPU:4 now
where the time goes in v4:
time: 68.8 us; the launch traced here: 68.7 us
  starting transfers between devices  29.8 us (43%)
  Pallas kernels  23.5 us (34%)
  waiting for transfers between devices  7.82 us (11%)
  local copies, waits for them, and re-layouts  5.02 us (7%)
  between operations  1.62 us (2%)
  other arithmetic  0.91 us (1%)
    pallas_call x1, Pallas kernels, serve(): pl.pallas_call(functools.partial(serve_kernel, peers, per_device, heads,...  9.76 us
    pallas_call x2, Pallas kernels, place(): pl.pallas_call(functools.partial(place_kernel, per_device, find, len(numb...  8.51 us
    ppermute x2, starting transfers between devices, total_but_y(): x = x + lax.ppermute(x, 'tp', [(i, i ^ hop) for i in range(ring)])  5.81 us
    ppermute x1, starting transfers between devices, shards(): far_rows = lax.ppermute(rows, 'dom', off_chip)  4.33 us
    ppermute x3, starting transfers between devices, parts_along_y(): parts.append(lax.ppermute(x, 'dom', pairs))  4.06 us
    ppermute x1, starting transfers between devices, shards(): first = lax.ppermute(sent, 'dom', off_chip)  4 us
    ppermute x1, starting transfers between devices, shards(): second = lax.ppermute(sent, 'dom', off_chip)  3.83 us
    ppermute x2, waiting for transfers between devices, total_but_y(): x = x + lax.ppermute(x, 'tp', [(i, i ^ hop) for i in range(ring)])  3.39 us
  transfers between devices with their start and end apart: 16, of which 8 were waited for; matrix products, arithmetic and copies ran while one was open for 3% of the time, Pallas kernels for 33%

profile of v4, /device:TPU:4, one launch (start us, length us, event | category | flops | bytes accessed | tf_op | source)
XLA Modules:
  0.0 68.7 jit_solution(14638946143293947009)
XLA Ops:
  0.6 1.0 %reshape.55.own = bf16[32,4096]{1,0:T(8,128)(2,1)S(1)} reshape(bf16[16,2,4096]{2,1,0:T(2,128)(2,1)} %param.21) | data formatting | bytes 524288 | tf_op jit(solution)/shard_map/reshape | solution.py:556
  1.7 4.3 %collective-permute-start.8 = (bf16[32,4096]{1,0:T(8,128)(2,1)S(1)}, bf16[32,4096]{1,0:T(8,128)(2,1)S(1)}, u32[]{:S(2)}, u32[]{:S(2)}) collective-permute-start(bf16[32,4096]{1,0:T(8,128)(2,1)S(1)} %reshape.55.own), channel_id=1, source_target_pairs={{4,8},{8,4},{12,16},{16,12},{20,24},{24,20},{28,32},{32,28},{36,40... | collective-permute-start | bytes 786440 | tf_op jit(solution)/shard_map/ppermute | solution.py:557
  6.1 0.7 copy-done.3
  6.8 1.7 %plan.1 = (s32[1]{0:T(128)}, s32[16]{0:T(128)S(1)}, s32[16]{0:T(128)S(1)}) custom-call(s32[512]{0:T(512)S(1)} %copy-done.3, s32[4,128]{1,0:T(4,128)S(1)} %bitcast.5), custom_call_target="tpu_custom_call" | custom-call | tf_op jit(solution)/shard_map/plan/pallas_call | solution.py:96
  8.6 2.7 %gather.17 = bf16[2,6,512,256]{3,2,1,0:T(8,128)(2,1)S(1)} custom-call(s32[16]{0:T(128)S(1)} %get-tuple-element.129.picks, bf16[2,16,512,256]{3,2,1,0:T(8,128)(2,1)} %cache.3), custom_call_target="tpu_custom_call" | custom-call | tf_op jit(solution)/shard_map/gather/pallas_call | solution.py:129
  11.4 0.1 collective-permute-done.8.far
  11.5 0.5 collective-permute-start.17
  11.9 4.0 %collective-permute-start.18 = (bf16[2,6,512,256]{3,2,1,0:T(8,128)(2,1)S(1)}, bf16[2,6,512,256]{3,2,1,0:T(8,128)(2,1)}, u32[]{:S(2)}, u32[]{:S(2)}) collective-permute-start(bf16[2,6,512,256]{3,2,1,0:T(8,128)(2,1)S(1)} %gather.17), channel_id=1, source_target_pairs={{4,8},{8,4},{12,16},{16,12},{20,24},{24,20},{28,32},{32,28},{36,40... | collective-permute-start | bytes 9437192 | tf_op jit(solution)/shard_map/ppermute | solution.py:561
  16.0 1.6 %copy-done.2 = bf16[4096,256]{1,0:T(8,128)(2,1)S(1)} copy-done((bf16[4096,256]{1,0:T(8,128)(2,1)S(1)}, bf16[4096,256]{1,0:T(8,128)(2,1)}, u32[]{:S(2)}) %copy-start.2) | copy-done | bytes 2097176
  17.6 9.8 %serve.1 = (bf16[32,256]{1,0:T(8,128)(2,1)S(1)}, bf16[32,256]{1,0:T(8,128)(2,1)S(1)}, bf16[256,128]{1,0:T(8,128)(2,1)S(1)}, bf16[512,128]{1,0:T(8,128)(2,1)S(1)}...) custom-call(s32[512]{0:T(512)S(1)} %copy-done.4, ...), custom_call_target="tpu_custom_call" | custom-call | tf_op jit(solution)/shard_map/serve/pallas_call | solution.py:452
  27.4 0.6 copy-done.10
  28.0 3.8 %collective-permute-start.10 = (bf16[2,2,512,256]{3,2,1,0:T(8,128)(2,1)}, bf16[2,2,512,256]{3,2,1,0:T(8,128)(2,1)}, u32[]{:S(2)}, u32[]{:S(2)}) collective-permute-start(bf16[2,2,512,256]{3,2,1,0:T(8,128)(2,1)} %get-tuple-element.133), channel_id=1, source_target_pairs={{4,8},{8,4},{12,16},{16,12},{20,24},{24,20},{28,32},{32,28},{36,40... | collective-permute-start | bytes 3145736 | tf_op jit(solution)/shard_map/ppermute | solution.py:569
  32.0 1.2 %collective-permute-done.11 = f32[32,16]{1,0:T(8,128)S(1)} collective-permute-done((f32[32,16]{1,0:T(8,128)S(1)}, f32[32,16]{1,0:T(8,128)S(1)}, u32[]{:S(2)}, u32[]{:S(2)}) %collective-permute-start.11) | collective-permute-done | bytes 2080 | tf_op jit(solution)/shard_map/ppermute | solution.py:517
  33.2 1.9 %collective-permute-start.12 = (f32[32,16]{1,0:T(8,128)S(1)}, f32[32,16]{1,0:T(8,128)S(1)}, u32[]{:S(2)}, u32[]{:S(2)}) collective-permute-start(f32[32,16]{1,0:T(8,128)S(1)} %add.31), channel_id=1, source_target_pairs={{0,1},{1,0},{2,3},{3,2},{4,5},{5,4},{6,7},{7,6},{8,9},{9,8},{10,11... | collective-permute-start | bytes 6152 | tf_op jit(solution)/shard_map/ppermute | solution.py:520
  35.1 1.8 %collective-permute-done.12 = f32[32,16]{1,0:T(8,128)S(1)} collective-permute-done((f32[32,16]{1,0:T(8,128)S(1)}, f32[32,16]{1,0:T(8,128)S(1)}, u32[]{:S(2)}, u32[]{:S(2)}) %collective-permute-start.12) | collective-permute-done | bytes 2080 | tf_op jit(solution)/shard_map/ppermute | solution.py:520
  36.9 3.9 %collective-permute-start.13 = (f32[32,16]{1,0:T(8,128)S(1)}, f32[32,16]{1,0:T(8,128)S(1)}, u32[]{:S(2)}, u32[]{:S(2)}) collective-permute-start(f32[32,16]{1,0:T(8,128)S(1)} %add.32), channel_id=1, source_target_pairs={{0,2},{1,3},{2,0},{3,1},{4,6},{5,7},{6,4},{7,5},{8,10},{9,11},{10,... | collective-permute-start | bytes 6152 | tf_op jit(solution)/shard_map/ppermute | solution.py:520
  40.9 1.6 %collective-permute-done.13 = f32[32,16]{1,0:T(8,128)S(1)} collective-permute-done((f32[32,16]{1,0:T(8,128)S(1)}, f32[32,16]{1,0:T(8,128)S(1)}, u32[]{:S(2)}, u32[]{:S(2)}) %collective-permute-start.13) | collective-permute-done | bytes 2080 | tf_op jit(solution)/shard_map/ppermute | solution.py:520
  42.5 2.9 %collective-permute-start.14 = (f32[32,16]{1,0:T(8,128)S(1)}, f32[32,16]{1,0:T(8,128)S(1)}, u32[]{:S(2)}, u32[]{:S(2)}) collective-permute-start(f32[32,16]{1,0:T(8,128)S(1)} %add.33), channel_id=1, source_target_pairs={{0,32},{4,100},{8,40},{12,108},{16,48},{20,116},{24,56},{28,124},{... | collective-permute-start | bytes 6152 | tf_op jit(solution)/shard_map/ppermute | solution.py:524
  45.5 0.1 eq.37
  46.4 0.4 collective-permute-done.14
  46.8 2.3 %collective-permute-start.15 = (f32[32,16]{1,0:T(8,128)S(1)}, f32[32,16]{1,0:T(8,128)S(1)}, u32[]{:S(2)}, u32[]{:S(2)}) collective-permute-start(f32[32,16]{1,0:T(8,128)S(1)} %collective-permute-done.14), channel_id=1, source_target_pairs={{0,32},{4,100},{8,40},{12,108},{16,48},{20,116},{24,56},{28,124},{... | collective-permute-start | bytes 6152 | tf_op jit(solution)/shard_map/ppermute | solution.py:525
  49.1 0.7 pad_maximum_fusion
  49.8 1.9 %collective-permute-start.20 = (bf16[256,128]{1,0:T(8,128)(2,1)S(1)}, bf16[256,128]{1,0:T(8,128)(2,1)S(1)}, u32[]{:S(2)}, u32[]{:S(2)}) collective-permute-start(bf16[256,128]{1,0:T(8,128)(2,1)S(1)} %split.9), channel_id=1, source_target_pairs={{0,8},{8,16},{12,4},{16,24},{20,12},{24,32},{28,20},{32,40},{36,28... | collective-permute-start | bytes 196616 | tf_op jit(solution)/shard_map/ppermute | solution.py:572
  51.8 1.5 %collective-permute-done.18.refs_3_ = bf16[2,6,512,256]{3,2,1,0:T(8,128)(2,1)} collective-permute-done((bf16[2,6,512,256]{3,2,1,0:T(8,128)(2,1)S(1)}, bf16[2,6,512,256]{3,2,1,0:T(8,128)(2,1)}, u32[]{:S(2)}, u32[]{:S(2)}) %collective-permute-start.18) | collective-permute-done | bytes 3145760 | tf_op jit(solution)/shard_map/ppermute | solution.py:561
  53.2 6.8 %place_first.1 = bf16[2,16,512,256]{3,2,1,0:T(8,128)(2,1)} custom-call(s32[512]{0:T(512)S(1)} %copy-done.4, s32[16]{0:T(128)S(1)} %get-tuple-element.128.refs_1_.refs_0_, bf16[2,16,512,256]{3,2,1,0:T(8,128)(2,1)} %collective-permute-done.17.refs_2_, bf16[2,6,512,256]{3,2,1,0:T(8,128)(2,1)} %collective-permute-done.18.refs_3_, ...), custom_call_target="tpu_custom_call", output_to_operand_aliasing={{}: (4, {})} | custom-call | tf_op jit(solution)/shard_map/place_first/pallas_call | solution.py:177
  60.2 4.0 %collective-permute-start.22 = (f32[32,16]{1,0:T(8,128)S(1)}, f32[32,16]{1,0:T(8,128)S(1)}, u32[]{:S(2)}, u32[]{:S(2)}) collective-permute-start(f32[32,16]{1,0:T(8,128)S(1)} %add_add_fusion.refs_0_), channel_id=1, source_target_pairs={{0,16},{4,20},{8,24},{12,28},{16,0},{20,4},{24,8},{28,12},{32,48},... | collective-permute-start | bytes 6152 | tf_op jit(solution)/shard_map/ppermute | solution.py:533
  64.2 0.1 fusion
  64.3 0.7 reshape.56
  65.0 0.2 collective-permute-done.10.refs_1_
  65.2 1.7 %place_more.17 = bf16[2,16,512,256]{3,2,1,0:T(8,128)(2,1)} custom-call(s32[16]{0:T(128)S(1)} %get-tuple-element.128.refs_1_.refs_0_, bf16[2,2,512,256]{3,2,1,0:T(8,128)(2,1)} %collective-permute-done.10.refs_1_, bf16[2,16,512,256]{3,2,1,0:T(8,128)(2,1)} %get-tuple-element.147.refs_2_), custom_call_target="tpu_custom_call", output_to_operand_aliasing={{}: (2, {})} | custom-call | tf_op jit(solution)/shard_map/place_more/pallas_call | solution.py:177
  66.9 1.0 %collective-permute-done.23.refs_3_ = f32[32,16]{1,0:T(8,128)S(1)} collective-permute-done((f32[32,16]{1,0:T(8,128)S(1)}, f32[32,16]{1,0:T(8,128)S(1)}, u32[]{:S(2)}, u32[]{:S(2)}) %collective-permute-start.23) | collective-permute-done | bytes 2080 | tf_op jit(solution)/shard_map/ppermute | solution.py:533
  67.9 0.8 %normalise.1 = f32[1,16]{1,0:T(1,128)} custom-call(f32[32,16]{1,0:T(8,128)S(1)} %add_add_fusion.refs_0_, f32[32,16]{1,0:T(8,128)S(1)} %collective-permute-done.21.refs_1_, f32[32,16]{1,0:T(8,128)S(1)} %collective-permute-done.22.refs_2_, f32[32,16]{1,0:T(8,128)S(1)} %collective-permute-done.23.refs_3_), custom_call_target="tpu_custom_call" | custom-call | tf_op jit(solution)/shard_map/normalise/pallas_call | solution.py:503
  (46 shorter events, 0.8 us)
Async XLA Ops:
  1.7 9.8 %collective-permute-start.8 = (bf16[32,4096]{1,0:T(8,128)(2,1)S(1)}, bf16[32,4096]{1,0:T(8,128)(2,1)S(1)}, u32[]{:S(2)}, u32[]{:S(2)}) collective-permute-start(bf16[32,4096]{1,0:T(8,128)(2,1)S(1)} %reshape.55.own), channel_id=1, source_target_pairs={{4,8},{8,4},{12,16},{16,12},{20,24},{24,20},{28,32},{32,28},{36,40... | collective-permute-start | bytes 786440 | tf_op jit(solution)/shard_map/ppermute | solution.py:557
  6.0 5.5 %collective-permute-start.9 = (bf16[32,4096]{1,0:T(8,128)(2,1)S(1)}, bf16[32,4096]{1,0:T(8,128)(2,1)S(1)}, u32[]{:S(2)}, u32[]{:S(2)}) collective-permute-start(bf16[32,4096]{1,0:T(8,128)(2,1)S(1)} %reshape.55.own), channel_id=1, source_target_pairs={{0,4},{4,0},{8,12},{12,8},{16,20},{20,16},{24,28},{28,24},{32,36},... | collective-permute-start | bytes 786440 | tf_op jit(solution)/shard_map/ppermute | solution.py:558
  6.1 0.7 copy-start.3
  8.5 7.4 %copy-start = (bf16[4096,1024]{1,0:T(8,128)(2,1)S(1)}, bf16[4096,1024]{1,0:T(8,128)(2,1)}, u32[]{:S(2)}) copy-start(bf16[4096,1024]{1,0:T(8,128)(2,1)} %wq.1) | copy-start | bytes 25165828
  8.5 7.4 %copy-start.1 = (bf16[4096,256]{1,0:T(8,128)(2,1)S(1)}, bf16[4096,256]{1,0:T(8,128)(2,1)}, u32[]{:S(2)}) copy-start(bf16[4096,256]{1,0:T(8,128)(2,1)} %wk.1) | copy-start | bytes 6291460
  8.5 7.4 %copy-start.4 = (s32[512]{0:T(512)S(1)}, s32[512]{0:T(512)}, u32[]{:S(2)}) copy-start(s32[512]{0:T(512)} %refs_0_.1) | copy-start | bytes 6148
  8.6 7.4 %copy-start.5 = (f32[32,128]{1,0:T(8,128)S(1)}, f32[32,128]{1,0:T(8,128)}, u32[]{:S(2)}) copy-start(f32[32,128]{1,0:T(8,128)} %constant.51.clone.cosine) | copy-start | bytes 49156
  8.6 7.4 %copy-start.6 = (f32[32,128]{1,0:T(8,128)S(1)}, f32[32,128]{1,0:T(8,128)}, u32[]{:S(2)}) copy-start(f32[32,128]{1,0:T(8,128)} %constant.52.clone.sine) | copy-start | bytes 49156
  8.6 7.4 %copy-start.7 = (f32[1024]{0:T(1024)S(1)}, f32[1024]{0:T(1024)}, u32[]{:S(2)}) copy-start(f32[1024]{0:T(1024)} %param.25) | copy-start | bytes 12292
  8.6 7.4 %copy-start.8 = (f32[16,2]{0,1:T(2,128)S(1)}, f32[16,2]{0,1:T(2,128)}, u32[]{:S(2)}) copy-start(f32[16,2]{0,1:T(2,128)} %param.27) | copy-start | bytes 388
  8.6 7.4 %copy-start.9 = (f32[16]{0:T(128)S(1)}, f32[16]{0:T(128)}, u32[]{:S(2)}) copy-start(f32[16]{0:T(128)} %parent_twist.1) | copy-start | bytes 196
  11.5 41.7 %collective-permute-start.17 = (bf16[2,16,512,256]{3,2,1,0:T(8,128)(2,1)}, bf16[2,16,512,256]{3,2,1,0:T(8,128)(2,1)}, u32[]{:S(2)}, u32[]{:S(2)}) collective-permute-start(bf16[2,16,512,256]{3,2,1,0:T(8,128)(2,1)} %cache.3), channel_id=1, source_target_pairs={{0,4},{4,0},{8,12},{12,8},{16,20},{20,16},{24,28},{28,24},{32,36},... | collective-permute-start | bytes 25165832 | tf_op jit(solution)/shard_map/ppermute | solution.py:563
  11.9 41.3 %collective-permute-start.18 = (bf16[2,6,512,256]{3,2,1,0:T(8,128)(2,1)S(1)}, bf16[2,6,512,256]{3,2,1,0:T(8,128)(2,1)}, u32[]{:S(2)}, u32[]{:S(2)}) collective-permute-start(bf16[2,6,512,256]{3,2,1,0:T(8,128)(2,1)S(1)} %gather.17), channel_id=1, source_target_pairs={{4,8},{8,4},{12,16},{16,12},{20,24},{24,20},{28,32},{32,28},{36,40... | collective-permute-start | bytes 9437192 | tf_op jit(solution)/shard_map/ppermute | solution.py:561
  16.0 1.6 %copy-start.2 = (bf16[4096,256]{1,0:T(8,128)(2,1)S(1)}, bf16[4096,256]{1,0:T(8,128)(2,1)}, u32[]{:S(2)}) copy-start(bf16[4096,256]{1,0:T(8,128)(2,1)} %wv.1) | copy-start | bytes 6291460
  27.4 0.7 copy-start.10
  28.0 37.2 %collective-permute-start.10 = (bf16[2,2,512,256]{3,2,1,0:T(8,128)(2,1)}, bf16[2,2,512,256]{3,2,1,0:T(8,128)(2,1)}, u32[]{:S(2)}, u32[]{:S(2)}) collective-permute-start(bf16[2,2,512,256]{3,2,1,0:T(8,128)(2,1)} %get-tuple-element.133), channel_id=1, source_target_pairs={{4,8},{8,4},{12,16},{16,12},{20,24},{24,20},{28,32},{32,28},{36,40... | collective-permute-start | bytes 3145736 | tf_op jit(solution)/shard_map/ppermute | solution.py:569
  31.9 1.3 %collective-permute-start.11 = (f32[32,16]{1,0:T(8,128)S(1)}, f32[32,16]{1,0:T(8,128)S(1)}, u32[]{:S(2)}, u32[]{:S(2)}) collective-permute-start(f32[32,16]{1,0:T(8,128)S(1)} %get-tuple-element.135), channel_id=1, source_target_pairs={{0,4},{4,0},{8,12},{12,8},{16,20},{20,16},{24,28},{28,24},{32,36},... | collective-permute-start | bytes 6152 | tf_op jit(solution)/shard_map/ppermute | solution.py:517
  33.2 3.7 %collective-permute-start.12 = (f32[32,16]{1,0:T(8,128)S(1)}, f32[32,16]{1,0:T(8,128)S(1)}, u32[]{:S(2)}, u32[]{:S(2)}) collective-permute-start(f32[32,16]{1,0:T(8,128)S(1)} %add.31), channel_id=1, source_target_pairs={{0,1},{1,0},{2,3},{3,2},{4,5},{5,4},{6,7},{7,6},{8,9},{9,8},{10,11... | collective-permute-start | bytes 6152 | tf_op jit(solution)/shard_map/ppermute | solution.py:520
  36.9 5.6 %collective-permute-start.13 = (f32[32,16]{1,0:T(8,128)S(1)}, f32[32,16]{1,0:T(8,128)S(1)}, u32[]{:S(2)}, u32[]{:S(2)}) collective-permute-start(f32[32,16]{1,0:T(8,128)S(1)} %add.32), channel_id=1, source_target_pairs={{0,2},{1,3},{2,0},{3,1},{4,6},{5,7},{6,4},{7,5},{8,10},{9,11},{10,... | collective-permute-start | bytes 6152 | tf_op jit(solution)/shard_map/ppermute | solution.py:520
  40.9 6.0 %collective-permute-start.19 = (bf16[512,128]{1,0:T(8,128)(2,1)}, bf16[512,128]{1,0:T(8,128)(2,1)S(1)}, u32[]{:S(2)}, u32[]{:S(2)}) collective-permute-start(bf16[512,128]{1,0:T(8,128)(2,1)} %copy-done.10), channel_id=1, source_target_pairs={{0,4},{4,0},{8,12},{12,8},{16,20},{20,16},{24,28},{28,24},{32,36},... | collective-permute-start | bytes 393224 | tf_op jit(solution)/shard_map/ppermute | solution.py:571
  42.5 4.3 %collective-permute-start.14 = (f32[32,16]{1,0:T(8,128)S(1)}, f32[32,16]{1,0:T(8,128)S(1)}, u32[]{:S(2)}, u32[]{:S(2)}) collective-permute-start(f32[32,16]{1,0:T(8,128)S(1)} %add.33), channel_id=1, source_target_pairs={{0,32},{4,100},{8,40},{12,108},{16,48},{20,116},{24,56},{28,124},{... | collective-permute-start | bytes 6152 | tf_op jit(solution)/shard_map/ppermute | solution.py:524
  46.8 3.0 %collective-permute-start.16 = (f32[32,16]{1,0:T(8,128)S(1)}, f32[32,16]{1,0:T(8,128)S(1)}, u32[]{:S(2)}, u32[]{:S(2)}) collective-permute-start(f32[32,16]{1,0:T(8,128)S(1)} %collective-permute-done.14), channel_id=1, source_target_pairs={{0,4},{4,0},{8,12},{12,8},{16,20},{20,16},{24,28},{28,24},{32,36},... | collective-permute-start | bytes 6152 | tf_op jit(solution)/shard_map/ppermute | solution.py:525
  46.8 4.9 %collective-permute-start.15 = (f32[32,16]{1,0:T(8,128)S(1)}, f32[32,16]{1,0:T(8,128)S(1)}, u32[]{:S(2)}, u32[]{:S(2)}) collective-permute-start(f32[32,16]{1,0:T(8,128)S(1)} %collective-permute-done.14), channel_id=1, source_target_pairs={{0,32},{4,100},{8,40},{12,108},{16,48},{20,116},{24,56},{28,124},{... | collective-permute-start | bytes 6152 | tf_op jit(solution)/shard_map/ppermute | solution.py:525
  49.8 14.4 %collective-permute-start.20 = (bf16[256,128]{1,0:T(8,128)(2,1)S(1)}, bf16[256,128]{1,0:T(8,128)(2,1)S(1)}, u32[]{:S(2)}, u32[]{:S(2)}) collective-permute-start(bf16[256,128]{1,0:T(8,128)(2,1)S(1)} %split.9), channel_id=1, source_target_pairs={{0,8},{8,16},{12,4},{16,24},{20,12},{24,32},{28,20},{32,40},{36,28... | collective-permute-start | bytes 196616 | tf_op jit(solution)/shard_map/ppermute | solution.py:572
  60.1 6.8 %collective-permute-start.21 = (f32[32,16]{1,0:T(8,128)S(1)}, f32[32,16]{1,0:T(8,128)S(1)}, u32[]{:S(2)}, u32[]{:S(2)}) collective-permute-start(f32[32,16]{1,0:T(8,128)S(1)} %add_add_fusion.refs_0_), channel_id=1, source_target_pairs={{0,8},{4,12},{8,16},{12,20},{16,24},{20,28},{24,0},{28,4},{32,40},... | collective-permute-start | bytes 6152 | tf_op jit(solution)/shard_map/ppermute | solution.py:533
  60.2 6.7 %collective-permute-start.22 = (f32[32,16]{1,0:T(8,128)S(1)}, f32[32,16]{1,0:T(8,128)S(1)}, u32[]{:S(2)}, u32[]{:S(2)}) collective-permute-start(f32[32,16]{1,0:T(8,128)S(1)} %add_add_fusion.refs_0_), channel_id=1, source_target_pairs={{0,16},{4,20},{8,24},{12,28},{16,0},{20,4},{24,8},{28,12},{32,48},... | collective-permute-start | bytes 6152 | tf_op jit(solution)/shard_map/ppermute | solution.py:533
  64.1 3.7 %collective-permute-start.23 = (f32[32,16]{1,0:T(8,128)S(1)}, f32[32,16]{1,0:T(8,128)S(1)}, u32[]{:S(2)}, u32[]{:S(2)}) collective-permute-start(f32[32,16]{1,0:T(8,128)S(1)} %add_add_fusion.refs_0_), channel_id=1, source_target_pairs={{0,24},{4,28},{8,0},{12,4},{16,8},{20,12},{24,16},{28,20},{32,56},... | collective-permute-start | bytes 6152 | tf_op jit(solution)/shard_map/ppermute | solution.py:533
